TPU v7x, 256 devices: a whole 4x4x8 slice. The times are simulated.
256 devices in a mesh: row: 16 (over z, x_hi), col: 16 (over x_lo, y, core).
Axes of the slice: x: 4 (x_hi: 2, x_lo: 2; x = x_hi * 2 + x_lo), y: 4, z: 8, core: 2. Of those that a mesh axis runs over, the one named last changes fastest.
Arguments:
- pair: bfloat16 [512, 512, 128], P('row', 'col'), may hold values from -6 to 6
- cotangent: bfloat16 [512, 512, 128], P('row', 'col'), may hold values from -6 to 6
- chain_counts: int32 [4], replicated, may hold values from 1 to 256, 512 in all
- crop_skip: int32 [4], replicated, may hold values from 0 to 31
- w_proj: bfloat16 [128, 256], replicated, may hold values from -0.5 to 0.5
- w_gate_in: bfloat16 [128, 256], replicated, may hold values from -0.5 to 0.5
- w_gate_out: bfloat16 [128, 128], replicated, may hold values from -0.5 to 0.5
- w_out: bfloat16 [128, 128], replicated, may hold values from -0.5 to 0.5
Outputs:
- updated: bfloat16 [512, 512, 128], P('row', 'col')
- grad_pair: bfloat16 [512, 512, 128], P('row', 'col')
- grad_proj: float32 [128, 256], replicated
- grad_gate_in: float32 [128, 256], replicated
- grad_gate_out: float32 [128, 128], replicated
- grad_out: float32 [128, 128], replicated
Inputs may be any that keep to these rules, and one draw needn't show every extreme that they name: `chain_counts`: the counts sum to 512.
All inputs are finite; a program needn't handle non-finite values.
Results may differ from a plain program's by a relative error of at most 0.0093.
Values may be sent and summed in bfloat16 or wider, within the bound.
A program may use at most 128 MiB of HBM per device.

v0:
```python
import jax
import jax.numpy as jnp
from jax import lax
from jax.sharding import PartitionSpec as P


def from_root(array, axis, root):
    mine = lax.axis_index(axis) == root
    return lax.psum(jnp.where(mine, array, jnp.zeros_like(array)), axis)


def residue_valid(index, chain_counts, crop_skip):
    ends = jnp.cumsum(chain_counts)
    starts = ends - chain_counts
    place = index[:, None]
    inside = (
        (place >= starts[None, :])
        & (place < ends[None, :])
        & (place - starts[None, :] >= crop_skip[None, :])
    )
    return jnp.any(inside, axis=1).astype(jnp.float32)


def shards(pair, cotangent, chain_counts, crop_skip, w_proj, w_gate_in, w_gate_out, w_out):
    row_count, col_count, channels = pair.shape
    hidden = w_out.shape[0]
    row_devices = lax.axis_size("row")
    col_devices = lax.axis_size("col")
    blocks_per = row_devices // col_devices
    row_at = lax.axis_index("row")
    col_at = lax.axis_index("col")
    total = row_count * row_devices
    row_index = row_at * row_count + jnp.arange(row_count, dtype=jnp.int32)
    col_index = col_at * col_count + jnp.arange(col_count, dtype=jnp.int32)
    valid_rows = residue_valid(row_index, chain_counts, crop_skip)
    valid_cols = residue_valid(col_index, chain_counts, crop_skip)
    cell_mask = (valid_rows[:, None] * valid_cols[None, :])[..., None]
    pair_float_input = pair.astype(jnp.float32)
    channel_mean = jnp.mean(pair_float_input, axis=-1, keepdims=True)
    var = jnp.mean((pair_float_input - channel_mean) ** 2, axis=-1, keepdims=True)
    inverse_deviation = 1.0 / jnp.sqrt(var + 1e-05)
    normalized_input = (pair_float_input - channel_mean) * inverse_deviation
    pair_input = normalized_input.astype(jnp.bfloat16)
    s_proj = jnp.dot(pair_input, w_proj, preferred_element_type=jnp.float32)
    s_gate = jnp.dot(pair_input, w_gate_in, preferred_element_type=jnp.float32)
    sig = jax.nn.sigmoid(s_gate)
    both = cell_mask * sig * s_proj
    left = both[..., :hidden].astype(jnp.bfloat16)
    right = both[..., hidden:].astype(jnp.bfloat16)
    right_local = lax.all_gather(right, "col", axis=1, tiled=True)
    blocks = from_root(right_local, "row", col_at * blocks_per + 0)
    tri = jnp.einsum(
        "ikh,jkh->ijh",
        lax.all_gather(left, "col", axis=1, tiled=True),
        blocks,
        preferred_element_type=jnp.float32,
    )
    tmean = jnp.mean(tri, axis=-1, keepdims=True)
    tvar = jnp.mean((tri - tmean) ** 2, axis=-1, keepdims=True)
    trstd = 1.0 / jnp.sqrt(tvar + 1e-05)
    that = (tri - tmean) * trstd
    tnorm = that.astype(jnp.bfloat16)
    gout = jax.nn.sigmoid(jnp.dot(pair_input, w_gate_out, preferred_element_type=jnp.float32))
    y_proj = jnp.dot(tnorm, w_out, preferred_element_type=jnp.float32)
    updated = (pair_float_input + gout * y_proj).astype(jnp.bfloat16)
    ct_f = cotangent.astype(jnp.float32)
    d_y = (ct_f * gout).astype(jnp.bfloat16)
    d_sgout = (ct_f * y_proj * gout * (1.0 - gout)).astype(jnp.bfloat16)
    d_tnorm = jnp.einsum("ijc,hc->ijh", d_y, w_out, preferred_element_type=jnp.float32)
    d_tri = (
        trstd
        * (
            d_tnorm
            - jnp.mean(d_tnorm, axis=-1, keepdims=True)
            - that * jnp.mean(d_tnorm * that, axis=-1, keepdims=True)
        )
    ).astype(jnp.bfloat16)
    grad_rows = lax.all_gather(d_tri, "col", axis=1, tiled=True)
    right_slab = lax.all_gather(right, "row", axis=0, tiled=True)
    grad_slab = lax.all_gather(d_tri, "row", axis=0, tiled=True)
    holder = from_root(grad_slab, "col", row_at // blocks_per)
    d_left = jnp.einsum("ijh,jkh->ikh", grad_rows, right_slab, preferred_element_type=jnp.float32)
    d_right = jnp.einsum(
        "ijh,ikh->jkh",
        holder,
        lax.all_gather(left, "row", axis=0, tiled=True),
        preferred_element_type=jnp.float32,
    )
    d_both = jnp.concatenate([d_left, d_right], axis=-1)
    d_proj = (d_both * cell_mask * sig).astype(jnp.bfloat16)
    d_gate = (d_both * cell_mask * s_proj * sig * (1.0 - sig)).astype(jnp.bfloat16)
    input_gradient = jnp.einsum("ijh,ch->ijc", d_proj, w_proj, preferred_element_type=jnp.float32)
    input_gradient = input_gradient + jnp.einsum(
        "ijh,ch->ijc", d_gate, w_gate_in, preferred_element_type=jnp.float32
    )
    input_gradient = input_gradient + jnp.einsum(
        "ijd,cd->ijc", d_sgout, w_gate_out, preferred_element_type=jnp.float32
    )
    gradient_before_norm = inverse_deviation * (
        input_gradient
        - jnp.mean(input_gradient, axis=-1, keepdims=True)
        - normalized_input * jnp.mean(input_gradient * normalized_input, axis=-1, keepdims=True)
    )
    grad_pair = (ct_f + gradient_before_norm).astype(jnp.bfloat16)
    term_proj = jnp.einsum("ijc,ijh->ch", pair_input, d_proj, preferred_element_type=jnp.float32)
    term_gate_in = jnp.einsum("ijc,ijh->ch", pair_input, d_gate, preferred_element_type=jnp.float32)
    term_gate_out = jnp.einsum(
        "ijc,ijd->cd", pair_input, d_sgout, preferred_element_type=jnp.float32
    )
    term_out = jnp.einsum("ijh,ijc->hc", tnorm, d_y, preferred_element_type=jnp.float32)
    summed = lax.psum((term_proj, term_gate_in, term_gate_out, term_out), ("row", "col"))
    scale = 1.0 / total
    return (
        updated,
        grad_pair,
        summed[0] * scale,
        summed[1] * scale,
        summed[2] * scale,
        summed[3] * scale,
    )


def solution(mesh):
    in_specs = (P("row", "col", None), P("row", "col", None), P(), P(), P(), P(), P(), P())
    out_specs = (P("row", "col", None), P("row", "col", None), P(), P(), P(), P())
    return jax.shard_map(shards, mesh=mesh, in_specs=in_specs, out_specs=out_specs, check_vma=False)
```

profile of v0, /device:TPU:1, one launch (start us, length us, event | category | flops | bytes accessed | tf_op | source)
XLA Modules:
  0.0 1081.3 jit_solution(4993273938482575296)
XLA Ops:
  7.2 0.0 all-gather.7.cloned.1.call-start
  7.2 0.9 reduce-window.8
  8.1 0.7 bitcast_subtract_fusion.1
  8.8 0.7 fusion.40
  9.5 1.2 convert_reduce_fusion
  10.7 1.3 fusion.14
  12.1 0.1 broadcast_multiply_fusion.4
  12.1 1.4 fusion.2
  13.6 0.9 copy-done.2
  14.5 1.5 multiply_convert_fusion.2
  16.0 0.9 fusion.51
  16.9 0.0 all-gather.9.cloned.1.call-start
  17.0 0.7 all-gather.9.cloned.1.call-update
  17.7 0.0 all-reduce.5.cloned.1.call-start
  17.7 43.5 %all-gather.7.cloned.1.call-done = bf16[32,512,128]{2,1,0:T(8,128)(2,1)} async-done(((bf16[32,32,128]{2,1,0:T(8,128)(2,1)}), bf16[32,512,128]{2,1,0:T(8,128)(2,1)}) %all-gather.7.cloned.1.call-update) | async-done | bytes 4194320 | tf_op jit(solution)/shard_map/all_gather | solution.py:50
  61.2 2.2 broadcast_select_fusion.1
  63.5 0.0 all-gather.17.cloned.1.call-start
  63.5 40.1 %all-gather.9.cloned.1.call-done = bf16[32,512,128]{2,1,0:T(8,128)(2,1)} async-done(((bf16[32,32,128]{2,1,0:T(8,128)(2,1)}), bf16[32,512,128]{2,1,0:T(8,128)(2,1)}) %all-gather.9.cloned.1.call-update) | async-done | bytes 4194320 | tf_op jit(solution)/shard_map/all_gather | solution.py:54
  103.6 8.0 copy.87
  111.6 198.2 %all-reduce.5.cloned.1.call-done = bf16[32,512,128]{2,1,0:T(8,128)(2,1)} async-done(((bf16[32,512,128]{2,1,0:T(8,128)(2,1)}), bf16[32,512,128]{2,1,0:T(8,128)(2,1)}) %all-reduce.5.cloned.1.call-update) | async-done | bytes 4194320 | tf_op jit(solution)/shard_map/psum | solution.py:9
  309.8 7.9 copy.86
  317.8 4.7 bitcast_reduce_fusion
  322.5 1.4 copy.88
  323.9 0.1 copy.90
  324.0 0.4 multiply_reduce_fusion.1
  324.4 0.5 fusion.30
  324.9 2.0 fusion.19
  326.8 0.8 fusion.50
  327.6 1.3 multiply_convert_fusion.3
  329.0 0.0 all-gather.11.cloned.1.call-start
  329.0 0.5 all-gather.11.cloned.1.call-update
  329.6 0.0 all-gather.15.cloned.1.call-start
  329.6 0.5 all-gather.15.cloned.1.call-update
  330.2 0.7 all-gather.13.cloned.1.call-update
  330.9 0.0 all-reduce.7.cloned.1.call-start
  331.0 97.0 %all-gather.17.cloned.1.call-done = bf16[512,32,128]{2,1,0:T(8,128)(2,1)} async-done(((bf16[32,32,128]{2,1,0:T(8,128)(2,1)}), bf16[512,32,128]{2,1,0:T(8,128)(2,1)}) %all-gather.17.cloned.1.call-update) | async-done | bytes 4194320 | tf_op jit(solution)/shard_map/all_gather | solution.py:80
  428.0 8.6 copy.98
  436.6 2.2 broadcast_select_fusion
  438.8 0.2 all-reduce.9.cloned.1.call-start
  439.1 87.9 %all-gather.11.cloned.1.call-done = bf16[512,32,128]{2,1,0:T(8,128)(2,1)} async-done(((bf16[32,32,128]{2,1,0:T(8,128)(2,1)}), bf16[512,32,128]{2,1,0:T(8,128)(2,1)}) %all-gather.11.cloned.1.call-update) | async-done | bytes 4194320 | tf_op jit(solution)/shard_map/all_gather | solution.py:79
  527.0 8.6 copy.95
  535.5 91.0 %all-gather.15.cloned.1.call-done = bf16[512,32,128]{2,1,0:T(8,128)(2,1)} async-done(((bf16[32,32,128]{2,1,0:T(8,128)(2,1)}), bf16[512,32,128]{2,1,0:T(8,128)(2,1)}) %all-gather.15.cloned.1.call-update) | async-done | bytes 4194320 | tf_op jit(solution)/shard_map/all_gather | solution.py:86
  626.6 8.6 copy.99
  635.2 1.2 convolution_bitcast_fusion.3
  636.4 1.2 convolution_bitcast_fusion.2
  637.6 30.9 %all-gather.13.cloned.1.call-done = bf16[32,512,128]{2,1,0:T(8,128)(2,1)} async-done(((bf16[32,32,128]{2,1,0:T(8,128)(2,1)}), bf16[32,512,128]{2,1,0:T(8,128)(2,1)}) %all-gather.13.cloned.1.call-update) | async-done | bytes 4194320 | tf_op jit(solution)/shard_map/all_gather | solution.py:78
  668.5 7.9 copy.96
  676.4 4.7 fusion.52
  681.1 1.4 copy.97
  682.5 122.1 %all-reduce.7.cloned.1.call-done = bf16[512,32,128]{0,1,2:T(8,128)(2,1)} async-done(((bf16[512,32,128]{0,1,2:T(8,128)(2,1)}), bf16[512,32,128]{0,1,2:T(8,128)(2,1)}) %all-reduce.7.cloned.1.call-update) | async-done | bytes 4194320 | tf_op jit(solution)/shard_map/psum | solution.py:9
  804.6 4.7 fusion.53
  809.3 2.2 copy.100
  811.5 2.0 multiply_convert_fusion
  813.6 1.2 convolution_bitcast_fusion.1
  814.8 0.3 fusion.23
  815.1 1.2 convolution_bitcast_fusion
  816.3 0.3 convolution_add_fusion.1
  816.6 0.8 fusion.49
  817.5 1.3 fusion.20
  818.8 249.9 %all-reduce.9.cloned.1.call-done = (f32[128,256]{1,0:T(8,128)}, f32[128,256]{1,0:T(8,128)}, f32[128,128]{1,0:T(8,128)}, f32[128,128]{1,0:T(8,128)}) async-done(((f32[128,256]{1,0:T(8,128)}, f32[128,256]{1,0:T(8,128)}, f32[128,128]{1,0:T(8,128)}, f32[128,128]{1,0:T(8,128)}), (f32[128,256]{1,0:T(8,128)}, f32[128,256]{1,0:T(8,128)}, f32[128,128]{1,0:T(8,128)}, ...) | async-done | bytes 393232 | tf_op jit(solution)/shard_map/psum | solution.py:111
  1068.7 1.6 broadcast_multiply_fusion
  1070.3 1.6 broadcast_multiply_fusion.1
  1071.8 1.5 broadcast_multiply_fusion.2
  1073.3 1.5 broadcast_multiply_fusion.3
  (30 shorter events, 0.2 us)
Async XLA Ops:
  7.2 7.4 copy-start
  7.2 7.3 copy-start.1
  7.2 54.0 %all-gather.7.cloned.1.call-start = ((), (), s32[]{:S(2)}) async-start(), calls=%async_computation | async-start | bytes 4456448 | tf_op jit(solution)/shard_map/all_gather | solution.py:50
  13.6 1.0 copy-start.2
  16.9 86.7 %all-gather.9.cloned.1.call-start = ((), (), s32[]{:S(2)}) async-start(), calls=%async_computation.2 | async-start | bytes 4456448 | tf_op jit(solution)/shard_map/all_gather | solution.py:54
  17.7 292.1 %all-reduce.5.cloned.1.call-start = ((), (), s32[]{:S(2)}) async-start(), calls=%async_computation.1 | async-start | bytes 8388608 | tf_op jit(solution)/shard_map/psum | solution.py:9
  63.5 364.5 %all-gather.17.cloned.1.call-start = ((), (), s32[]{:S(2)}) async-start(), calls=%async_computation.6 | async-start | bytes 4456448 | tf_op jit(solution)/shard_map/all_gather | solution.py:80
  317.8 6.6 copy-start.4
  322.5 2.4 copy-start.3
  329.0 198.0 %all-gather.11.cloned.1.call-start = ((), (), s32[]{:S(2)}) async-start(), calls=%async_computation.3 | async-start | bytes 4456448 | tf_op jit(solution)/shard_map/all_gather | solution.py:79
  329.6 297.0 %all-gather.15.cloned.1.call-start = ((), (), s32[]{:S(2)}) async-start(), calls=%async_computation.5 | async-start | bytes 4456448 | tf_op jit(solution)/shard_map/all_gather | solution.py:86
  330.2 338.4 %all-gather.13.cloned.1.call-start = ((), (), s32[]{:S(2)}) async-start(), calls=%async_computation.4 | async-start | bytes 4456448 | tf_op jit(solution)/shard_map/all_gather | solution.py:78
  330.9 473.7 %all-reduce.7.cloned.1.call-start = ((), (), s32[]{:S(2)}) async-start(), calls=%async_computation.7 | async-start | bytes 8388608 | tf_op jit(solution)/shard_map/psum | solution.py:9
  438.8 629.9 %all-reduce.9.cloned.1.call-start = ((), (), s32[]{:S(2)}) async-start(), calls=%async_computation.8 | async-start | bytes 786432 | tf_op jit(solution)/shard_map/psum | solution.py:111
  811.5 4.8 copy-start.5
  811.5 5.1 copy-start.6
Sparse Core Ops, SparseCore 0:
  17.1 44.1 all-gather.6
  63.6 39.9 all-gather.8
  106.3 203.4 all-reduce.4
  329.1 98.8 all-gather.16
  430.4 96.5 all-gather.10
  530.0 96.5 all-gather.14
  628.4 40.0 all-gather.12
  671.2 133.3 all-reduce.6
  817.6 251.0 all-reduce.8
where the time goes:
time: 1080 us
  waiting for transfers between devices  963 us (89%)
  local copies, waits for them, and re-layouts  56.6 us (5%)
  matrix products  26.5 us (2%)
  other arithmetic  20.5 us (2%)
  between operations  14.1 us (1%)
    psum x2, waiting for transfers between devices, from_root(): return lax.psum(jnp.where(mine, array, jnp.zeros_like(array)), axis)  320 us
    psum x1, waiting for transfers between devices, shards(): lax.psum((term_proj, term_gate_in, term_gate_out, term_out), ('row', 'col'))  250 us
    all_gather x1, waiting for transfers between devices, shards(): grad_slab = lax.all_gather(d_tri, 'row', axis=0, tiled=True)  97 us
    all_gather x1, waiting for transfers between devices, shards(): lax.all_gather(left, 'row', axis=0, tiled=True)  91 us
    all_gather x1, waiting for transfers between devices, shards(): right_slab = lax.all_gather(right, 'row', axis=0, tiled=True)  87.9 us
    all_gather x1, waiting for transfers between devices, shards(): right_local = lax.all_gather(right, 'col', axis=1, tiled=True)  43.5 us
    all_gather x1, waiting for transfers between devices, shards(): lax.all_gather(left, 'col', axis=1, tiled=True)  40.1 us
    all_gather x1, waiting for transfers between devices, shards(): grad_rows = lax.all_gather(d_tri, 'col', axis=1, tiled=True)  30.9 us
  transfers between devices with their start and end apart: 9, of which 9 were waited for; matrix products, arithmetic and copies ran while one was open for 5% of the time, Pallas kernels for 0%

commit v1 on v0

v1 whole, which is shorter than its diff:
```python
import functools

import jax
import jax.numpy as jnp
from jax import lax
from jax.experimental import pallas as pl
from jax.experimental.pallas import tpu as pltpu
from jax.sharding import PartitionSpec as P

MESH = pl.DeviceIdType.MESH
BF = jnp.bfloat16
F32 = jnp.float32


def enter(r, c, sem):
    barrier = pltpu.get_barrier_semaphore()

    def greet(s, _):
        pl.semaphore_signal(barrier, inc=1, device_id=(lax.rem(r + s, 16), c), device_id_type=MESH)
        pl.semaphore_signal(barrier, inc=1, device_id=(r, lax.rem(c + s, 16)), device_id_type=MESH)
        return 0

    lax.fori_loop(1, 16, greet, 0)
    pl.semaphore_wait(barrier, 30)

    def tell(s, _):
        pl.semaphore_signal(sem, inc=1, device_id=(r, lax.rem(c + s, 16)), device_id_type=MESH)
        return 0

    lax.fori_loop(1, 16, tell, 0)
    pl.semaphore_wait(sem, 15)


def to_channels(src, full, send_sem, recv_sem, swap_send, swap_recv, r, c):
    half = r // 8
    m = c // 2
    core = lax.rem(c, 2)
    slot = r * 16 + c
    own = r * 8 + m
    same = core == half

    @pl.when(same)
    def _():
        pltpu.make_async_copy(src.at[own], full.at[slot], recv_sem).start()

    @pl.when(jnp.logical_not(same))
    def _():
        pltpu.make_async_remote_copy(
            src_ref=src.at[own], dst_ref=full.at[slot], send_sem=send_sem, recv_sem=recv_sem,
            device_id=(r, m * 2 + half), device_id_type=MESH,
        ).start()

    def body(s, _):
        r2 = lax.rem(r + lax.rem(s, 16), 16)
        m2 = lax.rem(m + s // 16, 8)
        pltpu.make_async_remote_copy(
            src_ref=src.at[r2 * 8 + m2], dst_ref=full.at[slot], send_sem=send_sem, recv_sem=recv_sem,
            device_id=(r2, m2 * 2 + half), device_id_type=MESH,
        ).start()
        return 0

    lax.fori_loop(1, 128, body, 0)
    mine = full.at[pl.ds(core * 128, 128)]
    pltpu.make_async_copy(mine, mine, recv_sem).wait()
    swap = pltpu.make_async_remote_copy(
        src_ref=mine, dst_ref=mine, send_sem=swap_send, recv_sem=swap_recv,
        device_id=(r, m * 2 + 1 - core), device_id_type=MESH,
    )
    swap.start()

    @pl.when(same)
    def _():
        pltpu.make_async_copy(src.at[pl.ds(0, 127)], src.at[pl.ds(0, 127)], send_sem).wait()

    @pl.when(jnp.logical_not(same))
    def _():
        pltpu.make_async_copy(src, src, send_sem).wait()

    swap.wait()


def to_cells(src, dst, send_sem, recv_sem, r, c):
    m = c // 2
    core = lax.rem(c, 2)
    channel = r * 8 + m
    home = core == r // 8

    @pl.when(home)
    def _():
        pltpu.make_async_copy(src.at[lax.rem(r, 8) * 16 + c], dst.at[channel], recv_sem).start()

    @pl.when(jnp.logical_not(home))
    def _():
        r2 = core * 8 + lax.rem(r, 8)
        pltpu.make_async_remote_copy(
            src_ref=src.at[lax.rem(r, 8) * 16 + c], dst_ref=dst.at[channel], send_sem=send_sem, recv_sem=recv_sem,
            device_id=(r2, c), device_id_type=MESH,
        ).start()

    def body(s, _):
        q = lax.rem(r + lax.rem(s, 8), 8)
        c2 = lax.rem(c + s // 8, 16)
        pltpu.make_async_remote_copy(
            src_ref=src.at[q * 16 + c2], dst_ref=dst.at[channel], send_sem=send_sem, recv_sem=recv_sem,
            device_id=(core * 8 + q, c2), device_id_type=MESH,
        ).start()
        return 0

    lax.fori_loop(1, 128, body, 0)
    pltpu.make_async_copy(dst, dst, recv_sem).wait()

    @pl.when(home)
    def _():
        pltpu.make_async_copy(src.at[pl.ds(0, 127)], src.at[pl.ds(0, 127)], send_sem).wait()

    @pl.when(jnp.logical_not(home))
    def _():
        pltpu.make_async_copy(src, src, send_sem).wait()


def channels_kernel(src, full, dma, reg):
    r, c = lax.axis_index("row"), lax.axis_index("col")
    enter(r, c, reg.at[0])
    to_channels(src, full, dma.at[0], dma.at[1], dma.at[2], dma.at[3], r, c)


def cells_kernel(src, dst, dma, reg):
    r, c = lax.axis_index("row"), lax.axis_index("col")
    enter(r, c, reg.at[0])
    to_cells(src, dst, dma.at[0], dma.at[1], r, c)


def sum_kernel(src, out, got, part, tot, parts, dma, reg):
    r, c = lax.axis_index("row"), lax.axis_index("col")
    enter(r, c, reg.at[0])

    def scatter(s, _):
        c2 = lax.rem(c + s, 16)
        pltpu.make_async_remote_copy(
            src_ref=src.at[c2], dst_ref=got.at[c], send_sem=dma.at[0], recv_sem=dma.at[1],
            device_id=(r, c2), device_id_type=MESH,
        ).start()
        return 0

    pltpu.make_async_copy(src.at[c], got.at[c], dma.at[1]).start()
    lax.fori_loop(1, 16, scatter, 0)
    pltpu.make_async_copy(got, got, dma.at[1]).wait()
    part[...] = jnp.sum(got[...], axis=0)

    def share(s, _):
        r2 = lax.rem(r + s, 16)
        pltpu.make_async_remote_copy(
            src_ref=part, dst_ref=parts.at[r], send_sem=dma.at[2], recv_sem=dma.at[3],
            device_id=(r2, c), device_id_type=MESH,
        ).start()
        return 0

    pltpu.make_async_copy(part, parts.at[r], dma.at[3]).start()
    lax.fori_loop(1, 16, share, 0)
    pltpu.make_async_copy(parts, parts, dma.at[3]).wait()
    tot[...] = jnp.sum(parts[...], axis=0)

    def gather(s, _):
        c2 = lax.rem(c + s, 16)
        pltpu.make_async_remote_copy(
            src_ref=tot, dst_ref=out.at[c], send_sem=dma.at[4], recv_sem=dma.at[5],
            device_id=(r, c2), device_id_type=MESH,
        ).start()
        return 0

    pltpu.make_async_copy(tot, out.at[c], dma.at[5]).start()
    lax.fori_loop(1, 16, gather, 0)
    pltpu.make_async_copy(out, out, dma.at[5]).wait()
    most = got.at[pl.ds(0, 15)]
    for k in (0, 2, 4):
        pltpu.make_async_copy(most, most, dma.at[k]).wait()


def run(kernel, x, out_shape, cid, scratch=()):
    vmem = pl.BlockSpec(memory_space=pltpu.VMEM)
    return pl.pallas_call(
        kernel,
        out_shape=out_shape,
        in_specs=[vmem],
        out_specs=vmem,
        scratch_shapes=list(scratch) + [pltpu.SemaphoreType.DMA((6,)), pltpu.SemaphoreType.REGULAR((1,))],
        compiler_params=pltpu.CompilerParams(collective_id=cid, has_side_effects=True, vmem_limit_bytes=40 << 20),
    )(x)


def residue_valid(index, chain_counts, crop_skip):
    ends = jnp.cumsum(chain_counts)
    starts = ends - chain_counts
    place = index[:, None]
    inside = (
        (place >= starts[None, :])
        & (place < ends[None, :])
        & (place - starts[None, :] >= crop_skip[None, :])
    )
    return jnp.any(inside, axis=1).astype(F32)


def shards(pair, cotangent, chain_counts, crop_skip, w_proj, w_gate_in, w_gate_out, w_out):
    r, c = lax.axis_index("row"), lax.axis_index("col")
    core = lax.rem(c, 2)
    rows = r * 32 + jnp.arange(32, dtype=jnp.int32)
    cols = c * 32 + jnp.arange(32, dtype=jnp.int32)
    valid_rows = residue_valid(rows, chain_counts, crop_skip)
    valid_cols = residue_valid(cols, chain_counts, crop_skip)
    mask = (valid_rows[:, None] * valid_cols[None, :]).reshape(1024, 1)
    pf = pair.reshape(1024, 128).astype(F32)
    ct = cotangent.reshape(1024, 128).astype(F32)
    mean = jnp.mean(pf, axis=-1, keepdims=True)
    var = jnp.mean((pf - mean) ** 2, axis=-1, keepdims=True)
    rstd = 1.0 / jnp.sqrt(var + 1e-05)
    xhat = (pf - mean) * rstd
    x = xhat.astype(BF)
    s_proj = jnp.dot(x, w_proj, preferred_element_type=F32)
    s_gate = jnp.dot(x, w_gate_in, preferred_element_type=F32)
    sig = jax.nn.sigmoid(s_gate)
    both = (mask * sig * s_proj).astype(BF)
    message = both.T.reshape(2, 128, 8, 128).transpose(1, 0, 2, 3).reshape(128, 16, 128)
    full = run(channels_kernel, message, jax.ShapeDtypeStruct((256, 16, 128), BF), 1)

    def matrix(a):
        return a.reshape(16, 16, 8, 4, 32).transpose(0, 2, 3, 1, 4).reshape(512, 512)

    def unmatrix(a):
        return a.reshape(8, 8, 4, 16, 32).transpose(0, 3, 1, 2, 4).reshape(128, 8, 128)

    left = matrix(full[:, :8])
    right = matrix(full[:, 8:])
    left_half = lax.dynamic_slice(left, (core * 256, 0), (256, 512))
    tri_half = lax.dot_general(left_half, right, (((1,), (1,)), ((), ())), preferred_element_type=F32).astype(BF)
    tri = run(cells_kernel, unmatrix(tri_half), jax.ShapeDtypeStruct((128, 8, 128), BF), 2)
    tri = tri.reshape(128, 1024).T.astype(F32)
    tmean = jnp.mean(tri, axis=-1, keepdims=True)
    tvar = jnp.mean((tri - tmean) ** 2, axis=-1, keepdims=True)
    trstd = 1.0 / jnp.sqrt(tvar + 1e-05)
    that = (tri - tmean) * trstd
    tnorm = that.astype(BF)
    gout = jax.nn.sigmoid(jnp.dot(x, w_gate_out, preferred_element_type=F32))
    y = jnp.dot(tnorm, w_out, preferred_element_type=F32)
    updated = (pf + gout * y).astype(BF)
    d_y = (ct * gout).astype(BF)
    d_sgout = (ct * y * gout * (1.0 - gout)).astype(BF)
    d_tnorm = jnp.dot(d_y, w_out.T, preferred_element_type=F32)
    d_tri = (
        trstd
        * (
            d_tnorm
            - jnp.mean(d_tnorm, axis=-1, keepdims=True)
            - that * jnp.mean(d_tnorm * that, axis=-1, keepdims=True)
        )
    ).astype(BF)
    dfull = run(channels_kernel, d_tri.T.reshape(128, 8, 128), jax.ShapeDtypeStruct((256, 8, 128), BF), 3)
    dt = matrix(dfull)
    dt_rows = lax.dynamic_slice(dt, (core * 256, 0), (256, 512))
    dt_cols = lax.dynamic_slice(dt, (0, core * 256), (512, 256))
    d_left = jnp.dot(dt_rows, right, preferred_element_type=F32).astype(BF)
    d_right = lax.dot_general(dt_cols, left, (((0,), (0,)), ((), ())), preferred_element_type=F32).astype(BF)
    back = jnp.concatenate([unmatrix(d_left), unmatrix(d_right)], axis=1)
    back = run(cells_kernel, back, jax.ShapeDtypeStruct((128, 16, 128), BF), 4)
    d_both = back.reshape(128, 2, 1024).transpose(2, 1, 0).reshape(1024, 256).astype(F32)
    d_proj = (d_both * mask * sig).astype(BF)
    d_gate = (d_both * mask * s_proj * sig * (1.0 - sig)).astype(BF)
    d_x = (
        jnp.dot(d_proj, w_proj.T, preferred_element_type=F32)
        + jnp.dot(d_gate, w_gate_in.T, preferred_element_type=F32)
        + jnp.dot(d_sgout, w_gate_out.T, preferred_element_type=F32)
    )
    d_pair = rstd * (
        d_x - jnp.mean(d_x, axis=-1, keepdims=True) - xhat * jnp.mean(d_x * xhat, axis=-1, keepdims=True)
    )
    grad_pair = (ct + d_pair).astype(BF)
    t_proj = jnp.dot(x.T, d_proj, preferred_element_type=F32)
    t_gate = jnp.dot(x.T, d_gate, preferred_element_type=F32)
    t_gout = jnp.dot(x.T, d_sgout, preferred_element_type=F32)
    t_out = jnp.dot(tnorm.T, d_y, preferred_element_type=F32)
    terms = jnp.concatenate([t_proj, t_gate, t_gout, t_out], axis=1).reshape(16, 48, 128)
    scratch = [
        pltpu.VMEM((16, 48, 128), F32), pltpu.VMEM((48, 128), F32), pltpu.VMEM((48, 128), F32),
        pltpu.VMEM((16, 48, 128), F32),
    ]
    sums = run(sum_kernel, terms, jax.ShapeDtypeStruct((16, 48, 128), F32), 5, scratch)
    sums = sums.reshape(128, 768) * (1.0 / 512)
    shape = (32, 32, 128)
    return (
        updated.reshape(shape), grad_pair.reshape(shape),
        sums[:, :256], sums[:, 256:512], sums[:, 512:640], sums[:, 640:],
    )


def solution(mesh):
    in_specs = (P("row", "col", None), P("row", "col", None), P(), P(), P(), P(), P(), P())
    out_specs = (P("row", "col", None), P("row", "col", None), P(), P(), P(), P())
    return jax.shard_map(shards, mesh=mesh, in_specs=in_specs, out_specs=out_specs, check_vma=False)
```

time: 1080 us -> 189 us (0.17)
  waiting for transfers between devices: 963 us -> 0 us
  Pallas kernels: 0 us -> 124 us
  matrix products: 26.5 us -> 9.83 us
  local copies, waits for them, and re-layouts: 56.6 us -> 41.7 us
  between operations: 14.1 us -> 1.23 us
    psum x3 -> x0, waiting for transfers between devices: 570 us -> none  [the longest x2 320 us: from_root(): return lax.psum(jnp.where(mine, array, jnp.zeros_like(array)), axis)]
    all_gather x6 -> x0, waiting for transfers between devices: 390 us -> none  [the longest x1 97 us: shards(): grad_slab = lax.all_gather(d_tri, 'row', axis=0, tiled=True)]
    pallas_call x0 -> x5, Pallas kernels: none -> 124 us  [run(): pl.pallas_call(kernel, out_shape=out_shape, in_specs=[vmem], out_specs=vm...]
    all_gather x5 -> x0, local copies, waits for them, and re-layouts: 41.6 us -> none  [the longest x1 8.62 us: shards(): lax.all_gather(left, 'row', axis=0, tiled=True)]
    reshape x0 -> x22, local copies, waits for them, and re-layouts: none -> 35.6 us  [the longest x9 27 us: matrix(): a.reshape(16, 16, 8, 4, 32).transpose(0, 2, 3, 1, 4).reshape(512, 512)]
    dot_general x15, matrix products: 26.5 us -> 9.83 us  [the longest x1 1.44 us: shards(): lax.dot_general(dt_cols, left, (((0,), (0,)), ((), ())), preferred_elemen...]
  transfers between devices with their start and end apart: 9 -> 0, of which waited for: 9 -> 0; matrix products, arithmetic and copies ran while one was open for 5% -> 0% of each run, Pallas kernels for 0% -> 0%
where the time goes in v1:
time: 189 us; the launch traced here: 188 us
  Pallas kernels  124 us (66%)
  local copies, waits for them, and re-layouts  41.7 us (22%)
  other arithmetic  11.6 us (6%)
  matrix products  9.83 us (5%)
    pallas_call x5, Pallas kernels, run(): pl.pallas_call(kernel, out_shape=out_shape, in_specs=[vmem], out_specs=vm...  124 us
    reshape x9, local copies, waits for them, and re-layouts, matrix(): a.reshape(16, 16, 8, 4, 32).transpose(0, 2, 3, 1, 4).reshape(512, 512)  27 us
    reshape x9, local copies, waits for them, and re-layouts, unmatrix(): a.reshape(8, 8, 4, 16, 32).transpose(0, 3, 1, 2, 4).reshape(128, 8, 128)  7.75 us

profile of v1, /device:TPU:1, one launch (start us, length us, event | category | flops | bytes accessed | tf_op | source)
XLA Modules:
  0.0 188.4 jit_solution(6160962040165455174)
XLA Ops:
  0.7 0.8 reduce-window.8
  1.5 0.7 bitcast_subtract_fusion.3
  2.2 0.7 fusion.31
  2.9 0.1 broadcast_multiply_fusion.1
  3.0 0.1 mul.157
  3.1 1.2 convert_reduce_fusion
  4.2 1.3 fusion.16
  5.7 1.3 fusion.20
  7.0 1.3 fusion.2
  8.4 0.3 fusion.42
  8.7 0.7 copy-done.6
  9.4 0.2 fusion.11
  9.6 0.1 reshape.206
  9.7 0.5 copy.35
  10.2 31.4 %shard_map.127 = bf16[256,16,128]{2,1,0:T(8,128)(2,1)S(1)} custom-call(bf16[128,16,128]{2,1,0:T(8,128)(2,1)S(1)} %bitcast.114), custom_call_target="tpu_custom_call" | custom-call | tf_op jit(solution)/shard_map/pallas_call | solution.py:181
  41.6 1.1 fusion.39
  42.7 3.1 %reshape.208 = bf16[16,16,8,4,32]{4,3,2,1,0:T(4,128)(2,1)S(1)} reshape(bf16[256,8,128]{2,1,0:T(8,128)(2,1)} %get-tuple-element.18) | data formatting | bytes 1048576 | tf_op jit(solution)/shard_map/reshape | solution.py:226
  45.8 2.8 %copy.65 = bf16[16,16,8,4,32]{4,1,3,2,0:T(8,128)(2,1)} copy(bf16[16,16,8,4,32]{4,3,2,1,0:T(4,128)(2,1)S(1)} %reshape.208) | data formatting | bytes 1048576 | tf_op jit(solution)/shard_map/reshape | solution.py:226
  48.6 4.1 %reshape.209 = bf16[512,512]{1,0:T(8,128)(2,1)} reshape(bf16[16,8,4,16,32]{4,3,2,1,0:T(8,128)(2,1)} %bitcast.115) | data formatting | bytes 1048576 | tf_op jit(solution)/shard_map/reshape | solution.py:226
  52.7 3.1 %reshape.210 = bf16[16,16,8,4,32]{4,3,2,1,0:T(4,128)(2,1)S(1)} reshape(bf16[256,8,128]{2,1,0:T(8,128)(2,1)} %get-tuple-element.19) | data formatting | bytes 1048576 | tf_op jit(solution)/shard_map/reshape | solution.py:226
  55.8 2.8 %copy.64 = bf16[16,16,8,4,32]{4,1,3,2,0:T(8,128)(2,1)} copy(bf16[16,16,8,4,32]{4,3,2,1,0:T(4,128)(2,1)S(1)} %reshape.210) | data formatting | bytes 1048576 | tf_op jit(solution)/shard_map/reshape | solution.py:226
  58.6 3.4 %reshape.211 = bf16[512,512]{1,0:T(8,128)(2,1)S(1)} reshape(bf16[16,8,4,16,32]{4,3,2,1,0:T(8,128)(2,1)} %bitcast.116) | data formatting | bytes 1048576 | tf_op jit(solution)/shard_map/reshape | solution.py:226
  62.0 0.3 convolution_convert_fusion.2
  62.4 0.6 reshape.212
  63.0 1.4 copy.68
  64.4 2.0 %reshape.213.src = bf16[128,8,128]{2,1,0:T(8,128)(2,1)S(1)} reshape(bf16[8,16,8,4,32]{4,3,2,1,0:T(4,128)(2,1)} %bitcast.119) | data formatting | bytes 524288 | tf_op jit(solution)/shard_map/reshape | solution.py:229
  66.4 17.5 %shard_map.128 = bf16[128,8,128]{2,1,0:T(8,128)(2,1)S(1)} custom-call(bf16[128,8,128]{2,1,0:T(8,128)(2,1)S(1)} %reshape.213.src), custom_call_target="tpu_custom_call" | custom-call | tf_op jit(solution)/shard_map/pallas_call | solution.py:181
  84.0 0.2 copy.49
  84.2 0.1 convert_reduce_fusion.1
  84.3 0.4 multiply_reduce_fusion
  84.7 0.3 fusion.36
  85.0 1.3 fusion.9
  86.3 0.5 fusion.35
  86.8 0.5 fusion.38
  87.3 0.5 fusion.13
  87.8 0.2 copy.50.src
  88.0 19.2 %shard_map.129 = bf16[256,8,128]{2,1,0:T(8,128)(2,1)S(1)} custom-call(bf16[128,8,128]{2,1,0:T(8,128)(2,1)S(1)} %copy.50.src), custom_call_target="tpu_custom_call" | custom-call | tf_op jit(solution)/shard_map/pallas_call | solution.py:181
  107.2 1.9 %reshape.216 = bf16[16,16,8,4,32]{4,3,2,1,0:T(4,128)(2,1)} reshape(bf16[256,8,128]{2,1,0:T(8,128)(2,1)S(1)} %shard_map.129) | data formatting | bytes 1048576 | tf_op jit(solution)/shard_map/reshape | solution.py:226
  109.1 3.1 %copy.63 = bf16[16,16,8,4,32]{4,1,3,2,0:T(8,128)(2,1)S(1)} copy(bf16[16,16,8,4,32]{4,3,2,1,0:T(4,128)(2,1)} %reshape.216) | data formatting | bytes 1048576 | tf_op jit(solution)/shard_map/reshape | solution.py:226
  112.1 2.8 %reshape.217 = bf16[512,512]{1,0:T(8,128)(2,1)} reshape(bf16[16,8,4,16,32]{4,3,2,1,0:T(8,128)(2,1)S(1)} %bitcast.117) | data formatting | bytes 1048576 | tf_op jit(solution)/shard_map/reshape | solution.py:226
  114.9 1.4 convolution_convert_fusion.1
  116.3 0.6 reshape.218
  116.9 0.4 copy.67
  117.4 1.2 reshape.219
  118.6 1.4 convolution_convert_fusion
  120.0 0.6 reshape.220
  120.6 0.4 copy.66
  121.1 0.5 reshape.221
  121.6 1.0 pad_maximum_fusion.src
  122.7 23.4 %shard_map.130 = bf16[128,16,128]{2,1,0:T(8,128)(2,1)S(1)} custom-call(bf16[128,16,128]{2,1,0:T(8,128)(2,1)S(1)} %pad_maximum_fusion.src), custom_call_target="tpu_custom_call" | custom-call | tf_op jit(solution)/shard_map/pallas_call | solution.py:181
  146.1 0.5 reshape.228
  146.6 2.0 %copy.44 = f32[1024,2,128]{2,1,0:T(2,128)} copy(f32[1024,2,128]{0,1,2:T(2,128)S(1)} %bitcast.122) | data formatting | bytes 2097152 | tf_op jit(solution)/shard_map/convert_element_type | solution.py:264
  148.6 1.9 %multiply_convert_fusion.1 = (bf16[1024,256]{1,0:T(8,128)(2,1)S(1)}, bf16[1024,256]{1,0:T(8,128)(2,1)S(1)}) fusion(f32[1024,256]{1,0:T(8,128)} %copy-done.6, f32[1024,256]{1,0:T(8,128)S(1)} %fusion.42, f32[128,8,2,128]{3,2,1,0:T(2,128)} %bitcast.118, f32[1024]{0:T(1024)S(1)} %mul.157), kind=kLoop, calls=%fused_computation.21 | loop fusion | flops 2097152 | bytes 4198400 | tf_op jit(solution)/shard_map/convert_element_type | solution.py:266
  150.5 0.3 fusion.44
  150.8 0.3 fusion.45
  151.1 0.3 fusion.46
  151.4 32.4 %shard_map.131 = f32[16,48,128]{2,1,0:T(8,128)S(1)} custom-call(f32[16,48,128]{2,1,0:T(8,128)S(1)} %reshape.223.src), custom_call_target="tpu_custom_call" | custom-call | tf_op jit(solution)/shard_map/pallas_call | solution.py:181
  183.9 0.1 mul.187
  184.0 0.7 fusion.41
  184.7 0.7 fusion.40
  185.3 0.3 fusion.43
  185.6 0.3 convolution_add_fusion.1
  185.9 1.1 fusion.37
  187.1 1.3 fusion.10
  (47 shorter events, 0.4 us)
Async XLA Ops:
  0.6 7.8 %copy-start = (bf16[128,256]{1,0:T(8,128)(2,1)S(1)}, bf16[128,256]{1,0:T(8,128)(2,1)}, u32[]{:S(2)}) copy-start(bf16[128,256]{1,0:T(8,128)(2,1)} %param.12) | copy-start | bytes 196612
  7.0 1.4 copy-start.2
  8.4 1.0 copy-start.6
  58.6 3.4 %copy-start.7 = (bf16[512,512]{1,0:T(8,128)(2,1)S(1)}, bf16[512,512]{1,0:T(8,128)(2,1)}, u32[]{:S(2)}) copy-start(bf16[512,512]{1,0:T(8,128)(2,1)} %reshape.209) | copy-start | bytes 1572868
  62.0 2.4 %copy-start.5 = (bf16[512,512]{1,0:T(8,128)(2,1)}, bf16[512,512]{1,0:T(8,128)(2,1)S(1)}, u32[]{:S(2)}) copy-start(bf16[512,512]{1,0:T(8,128)(2,1)S(1)} %reshape.211) | copy-start | bytes 1572868
  64.4 20.3 %copy-start.12 = (bf16[128,128]{1,0:T(8,128)(2,1)S(1)}, bf16[128,128]{1,0:T(8,128)(2,1)}, u32[]{:S(2)}) copy-start(bf16[128,128]{1,0:T(8,128)(2,1)} %param.15) | copy-start | bytes 98308
  66.4 18.6 %copy-start.1 = (bf16[32,32,128]{2,1,0:T(8,128)(2,1)S(1)}, bf16[32,32,128]{2,1,0:T(8,128)(2,1)}, u32[]{:S(2)}) copy-start(bf16[32,32,128]{2,1,0:T(8,128)(2,1)} %param.8) | copy-start | bytes 786436
  66.4 18.6 %copy-start.3 = (bf16[1024,128]{1,0:T(8,128)(2,1)S(1)}, bf16[1024,128]{1,0:T(8,128)(2,1)}, u32[]{:S(2)}) copy-start(bf16[1024,128]{1,0:T(8,128)(2,1)} %copy-done.2) | copy-start | bytes 786436
  66.4 18.6 %copy-start.10 = (bf16[32,32,128]{2,1,0:T(8,128)(2,1)S(1)}, bf16[32,32,128]{2,1,0:T(8,128)(2,1)}, u32[]{:S(2)}) copy-start(bf16[32,32,128]{2,1,0:T(8,128)(2,1)} %param.9) | copy-start | bytes 786436
  66.4 18.6 %copy-start.14 = (bf16[128,128]{1,0:T(8,128)(2,1)S(1)}, bf16[128,128]{1,0:T(8,128)(2,1)}, u32[]{:S(2)}) copy-start(bf16[128,128]{1,0:T(8,128)(2,1)} %param.14) | copy-start | bytes 98308
  148.6 1.9 %copy-start.4 = (bf16[1024,128]{1,0:T(8,128)(2,1)S(1)}, bf16[1024,128]{1,0:T(8,128)(2,1)}, u32[]{:S(2)}) copy-start(bf16[1024,128]{1,0:T(8,128)(2,1)} %copy-done.2) | copy-start | bytes 786436
  148.6 2.5 %copy-start.8 = (bf16[1024,128]{1,0:T(8,128)(2,1)S(1)}, bf16[1024,128]{1,0:T(8,128)(2,1)}, u32[]{:S(2)}) copy-start(bf16[1024,128]{1,0:T(8,128)(2,1)} %get-tuple-element.16) | copy-start | bytes 786436
  151.4 34.2 %copy-start.13 = (bf16[128,256]{1,0:T(8,128)(2,1)S(1)}, bf16[128,256]{1,0:T(8,128)(2,1)}, u32[]{:S(2)}) copy-start(bf16[128,256]{1,0:T(8,128)(2,1)} %param.13) | copy-start | bytes 196612
  183.8 2.1 %copy-start.9 = (bf16[1024,128]{1,0:T(8,128)(2,1)S(1)}, bf16[1024,128]{1,0:T(8,128)(2,1)}, u32[]{:S(2)}) copy-start(bf16[1024,128]{1,0:T(8,128)(2,1)} %get-tuple-element.16) | copy-start | bytes 786436
  183.9 2.1 %copy-start.15 = (bf16[128,128]{1,0:T(8,128)(2,1)S(1)}, bf16[128,128]{1,0:T(8,128)(2,1)}, u32[]{:S(2)}) copy-start(bf16[128,128]{1,0:T(8,128)(2,1)} %param.14) | copy-start | bytes 98308
  185.3 1.7 copy-start.11

commit v2 on v0

v2 whole, which is shorter than its diff:
```python
import jax
import jax.numpy as jnp
from jax import lax
from jax.experimental import pallas as pl
from jax.experimental.pallas import tpu as pltpu
from jax.sharding import PartitionSpec as P

MESH = pl.DeviceIdType.MESH
BF = jnp.bfloat16
F32 = jnp.float32
EPS = 1e-05


def dot(a, b, dims=((1,), (0,))):
    return lax.dot_general(a, b, (dims, ((), ())), preferred_element_type=F32)


def greet(r, c):
    barrier = pltpu.get_barrier_semaphore()

    def body(s, _):
        pl.semaphore_signal(barrier, inc=1, device_id=(lax.rem(r + s, 16), c), device_id_type=MESH)
        pl.semaphore_signal(barrier, inc=1, device_id=(r, lax.rem(c + s, 16)), device_id_type=MESH)
        return 0

    lax.fori_loop(1, 16, body, 0)


def tell(r, c, sem):
    pl.semaphore_wait(pltpu.get_barrier_semaphore(), 30)

    def body(s, _):
        pl.semaphore_signal(sem, inc=1, device_id=(r, lax.rem(c + s, 16)), device_id_type=MESH)
        return 0

    lax.fori_loop(1, 16, body, 0)


def remote(src, dst, send, recv, device):
    return pltpu.make_async_remote_copy(
        src_ref=src, dst_ref=dst, send_sem=send, recv_sem=recv, device_id=device, device_id_type=MESH
    )


def arrived(buf, sem):
    pltpu.make_async_copy(buf, buf, sem).wait()


def to_channels(src, dst, send, recv, r, c):
    half, m, core = r // 8, c // 2, lax.rem(c, 2)
    r8 = lax.rem(r, 8)
    own = r * 8 + m

    @pl.when(core == half)
    def _():
        pltpu.make_async_copy(src.at[own], dst.at[r8, c], recv).start()

    @pl.when(core != half)
    def _():
        remote(src.at[own], dst.at[r8, c], send, recv, (r, m * 2 + half)).start()

    def body(s, _):
        r2 = lax.rem(r + lax.rem(s, 16), 16)
        m2 = lax.rem(m + s // 16, 8)
        remote(src.at[r2 * 8 + m2], dst.at[r8, c], send, recv, (r2, m2 * 2 + half)).start()
        return 0

    lax.fori_loop(1, 128, body, 0)


def to_cells(src, dst, send, recv, r, c):
    half, m, core = r // 8, c // 2, lax.rem(c, 2)
    r8 = lax.rem(r, 8)
    channel = r * 8 + m

    @pl.when(core == half)
    def _():
        pltpu.make_async_copy(src.at[r8, c], dst.at[channel], recv).start()

    @pl.when(core != half)
    def _():
        remote(src.at[r8, c], dst.at[channel], send, recv, (core * 8 + r8, c)).start()

    def body(s, _):
        q = lax.rem(r + lax.rem(s, 8), 8)
        c2 = lax.rem(c + s // 8, 16)
        remote(src.at[q, c2], dst.at[channel], send, recv, (core * 8 + q, c2)).start()
        return 0

    lax.fori_loop(1, 128, body, 0)


def sent(src, send, r, c):
    same = r // 8 == lax.rem(c, 2)

    @pl.when(same)
    def _():
        arrived(src.at[pl.ds(0, 127)], send)

    @pl.when(jnp.logical_not(same))
    def _():
        arrived(src, send)


def along_col(pick, dst, send, recv, r, c):
    pltpu.make_async_copy(pick(c), dst.at[c], recv).start()

    def body(s, _):
        c2 = lax.rem(c + s, 16)
        remote(pick(c2), dst.at[c], send, recv, (r, c2)).start()
        return 0

    lax.fori_loop(1, 16, body, 0)


def along_row(src, dst, send, recv, r, c):
    pltpu.make_async_copy(src, dst.at[r], recv).start()

    def body(s, _):
        remote(src, dst.at[r], send, recv, (lax.rem(r + s, 16), c)).start()
        return 0

    lax.fori_loop(1, 16, body, 0)


def valid_of(place, counts, skip):
    start = jnp.int32(0)
    valid = jnp.zeros(place.shape, F32)
    for n in range(counts.shape[0]):
        end = start + counts[n]
        inside = (place >= start) & (place < end) & (place - start >= skip[n])
        valid = jnp.where(inside, 1.0, valid)
        start = end
    return valid


def kernel(
    counts, skip, pair, cot, w_proj, w_gin, w_gout, w_out,
    upd, gpair, g_proj, g_gin, g_gout, g_out,
    wp_t, wg_t, wgo_t, wo_t, perm,
    xh, xb, rstd, pt, ctt, gate, slope, go, dgo, dtn, dyb, tnb, dsb, dpb, dgb,
    f_left, f_right, f_mat, left, right, dmat, partial, got,
    m_r, m_l, m_t, m_d, m_dl, m_dr,
    b_r, b_l, b_t, b_d, b_dl, b_dr,
    e_src, e_got, e_part, e_parts, e_tot, e_out,
    s_src, s_got, s_part, s_parts, s_tot, s_out,
    send, recv, reg,
):
    r, c = lax.axis_index("row"), lax.axis_index("col")
    core = lax.rem(c, 2)
    sibling = (r, c + 1 - 2 * core)
    greet(r, c)

    wp_t[...] = w_proj[...].astype(F32).T.astype(BF)
    wg_t[...] = w_gin[...].astype(F32).T.astype(BF)
    wgo_t[...] = w_gout[...].astype(F32).T.astype(BF)
    wo_t[...] = w_out[...].astype(F32).T.astype(BF)
    i0 = lax.broadcasted_iota(jnp.int32, (128, 128), 0)
    i1 = lax.broadcasted_iota(jnp.int32, (128, 128), 1)
    eye = jnp.where(i0 == i1, 1.0, 0.0).astype(BF)

    tell(r, c, reg.at[0])

    def forward(q, _):
        p = pair[pl.ds(q * 4, 4)].reshape(128, 128)
        p_t = dot(eye, p, ((1,), (1,)))
        pt[q] = p_t
        mean = jnp.mean(p_t, axis=0, keepdims=True)
        dev = p_t - mean
        var = jnp.mean(dev * dev, axis=0, keepdims=True)
        rs = 1.0 / jnp.sqrt(var + EPS)
        x_f = dev * rs
        x = x_f.astype(BF)
        xh[q] = x_f
        rstd[q] = jnp.broadcast_to(rs, (8, 128))
        at = pl.ds(pl.multiple_of(q * 128, 128), 128)
        xb[:, at] = x
        s = dot(wp_t[...], x)
        sig = jax.nn.sigmoid(dot(wg_t[...], x))
        lane = lax.broadcasted_iota(jnp.int32, (1, 128), 1)
        mask = valid_of(r * 32 + q * 4 + lane // 32, counts, skip) * valid_of(c * 32 + lane % 32, counts, skip)
        open_ = mask * sig
        both = open_ * s
        gate[q] = open_
        slope[q] = both * (1.0 - sig)
        f_left[pl.ds(q, 128, stride=8), :] = both[:128]
        f_right[pl.ds(q, 128, stride=8), :] = both[128:]
        return 0

    lax.fori_loop(0, 8, forward, 0)
    m_r[...] = f_right[...].reshape(128, 8, 128).astype(BF)
    pl.semaphore_wait(reg.at[0], 15)
    to_channels(m_r, b_r, send.at[0], recv.at[0], r, c)
    m_l[...] = f_left[...].reshape(128, 8, 128).astype(BF)
    to_channels(m_l, b_l, send.at[1], recv.at[1], r, c)

    j0 = lax.broadcasted_iota(jnp.int32, (512, 512), 0)
    j1 = lax.broadcasted_iota(jnp.int32, (512, 512), 1)
    swapped = (j0 % 128) // 32 * 128 + j0 // 128 * 32 + j0 % 32
    perm[...] = jnp.where(swapped == j1, 1.0, 0.0).astype(BF)

    def before(q, _):
        at = pl.ds(pl.multiple_of(q * 128, 128), 128)
        ct = dot(eye, cot[pl.ds(q * 4, 4)].reshape(128, 128), ((1,), (1,)))
        ctt[q] = ct
        g = jax.nn.sigmoid(dot(wgo_t[...], xb[:, at]))
        go[q] = g
        dy_f = ct * g
        dgo[q] = dy_f * (1.0 - g)
        dy = dy_f.astype(BF)
        dyb[:, at] = dy
        dt = dot(w_out[...], dy)
        dtn[q] = dt - jnp.mean(dt, axis=0, keepdims=True)
        return 0

    lax.fori_loop(0, 8, before, 0)

    def matrix(buf, out):
        rows = []
        for g in range(4):
            cols = [buf[:, 4 * g + n].astype(F32).reshape(64, 128).astype(BF) for n in range(4)]
            rows.append(jnp.concatenate(cols, axis=1))
        o = dot(jnp.concatenate(rows, axis=0), perm[...])
        for g in range(4):
            for a in range(4):
                f_mat[pl.ds(g * 256 + a, 64, stride=4), :] = o[g * 64:(g + 1) * 64, a * 128:(a + 1) * 128]
        for g in range(4):
            out[:, g * 128:(g + 1) * 128] = f_mat[g * 256:(g + 1) * 256].astype(BF)

    def messages(mat, out):
        for g in range(4):
            f_mat[g * 256:(g + 1) * 256] = mat[:, g * 128:(g + 1) * 128]
        rows = []
        for g in range(4):
            cols = [f_mat[pl.ds(g * 256 + a, 64, stride=4), :].astype(BF) for a in range(4)]
            rows.append(jnp.concatenate(cols, axis=1))
        o = dot(jnp.concatenate(rows, axis=0), perm[...])
        for g in range(4):
            for n in range(4):
                out[:, 4 * g + n] = o[g * 64:(g + 1) * 64, n * 128:(n + 1) * 128].reshape(8, 8, 128).astype(BF)

    arrived(b_r, recv.at[0])
    mine = right.at[pl.ds(pl.multiple_of(core * 256, 256), 256)]
    matrix(b_r, mine)
    swap = remote(mine, mine, send.at[6], recv.at[6], sibling)
    swap.start()
    arrived(b_l, recv.at[1])
    matrix(b_l, left)
    swap.wait_recv()
    messages(dot(left[...], right[...], ((1,), (1,))), m_t)
    to_cells(m_t, b_t, send.at[2], recv.at[2], r, c)
    arrived(b_t, recv.at[2])
    f_left[...] = b_t[...].astype(F32).reshape(1024, 128)

    def middle(q, _):
        at = pl.ds(pl.multiple_of(q * 128, 128), 128)
        t = f_left[pl.ds(q, 128, stride=8), :]
        dev = t - jnp.mean(t, axis=0, keepdims=True)
        rs = 1.0 / jnp.sqrt(jnp.mean(dev * dev, axis=0, keepdims=True) + EPS)
        that = dev * rs
        tnb[:, at] = that.astype(BF)
        d = dtn[q]
        f_right[pl.ds(q, 128, stride=8), :] = rs * (d - that * jnp.mean(d * that, axis=0, keepdims=True))
        return 0

    lax.fori_loop(0, 8, middle, 0)
    m_d[...] = f_right[...].reshape(128, 8, 128).astype(BF)
    to_channels(m_d, b_d, send.at[3], recv.at[3], r, c)

    def after(q, _):
        at = pl.ds(pl.multiple_of(q * 128, 128), 128)
        y = dot(wo_t[...], tnb[:, at])
        dsb[:, at] = (dgo[q] * y).astype(BF)
        u = (pt[q] + go[q] * y).astype(BF)
        upd[pl.ds(q * 4, 4)] = dot(u, eye, ((0,), (0,))).astype(BF).reshape(4, 32, 128)
        return 0

    lax.fori_loop(0, 8, after, 0)
    e_src[pl.ds(0, 8)] = dot(xb[...], dsb[...], ((1,), (1,))).reshape(8, 16, 128)
    e_src[pl.ds(8, 8)] = dot(tnb[...], dyb[...], ((1,), (1,))).reshape(8, 16, 128)
    along_col(lambda n: e_src.at[n], e_got, send.at[7], recv.at[7], r, c)

    arrived(b_d, recv.at[3])
    matrix(b_d, dmat)
    theirs = pl.ds(pl.multiple_of((1 - core) * 256, 256), 256)
    ours = pl.ds(pl.multiple_of(core * 256, 256), 256)
    partial[...] = dot(dmat[:, theirs], left[...], ((0,), (0,)))
    cross = remote(partial, got, send.at[8], recv.at[8], sibling)
    cross.start()
    messages(dot(dmat[...], right[...]), m_dl)
    to_cells(m_dl, b_dl, send.at[4], recv.at[4], r, c)
    part = dot(dmat[:, ours], left[...], ((0,), (0,)))
    cross.wait_recv()
    messages(part + got[...], m_dr)
    to_cells(m_dr, b_dr, send.at[5], recv.at[5], r, c)

    arrived(e_got, recv.at[7])
    e_part[...] = jnp.sum(e_got[...], axis=0)
    along_row(e_part, e_parts, send.at[9], recv.at[9], r, c)

    def back(lo, f):
        def body(q, _):
            at = pl.ds(pl.multiple_of(q * 128, 128), 128)
            d = f[pl.ds(q, 128, stride=8), :]
            dpb[lo:lo + 128, at] = (d * gate[q, lo:lo + 128]).astype(BF)
            dgb[lo:lo + 128, at] = (d * slope[q, lo:lo + 128]).astype(BF)
            return 0

        lax.fori_loop(0, 8, body, 0)
        n = lo // 32
        s_src[pl.ds(n, 4)] = dot(xb[...], dpb[lo:lo + 128, :], ((1,), (1,))).reshape(4, 32, 128)
        s_src[pl.ds(8 + n, 4)] = dot(xb[...], dgb[lo:lo + 128, :], ((1,), (1,))).reshape(4, 32, 128)

    arrived(b_dl, recv.at[4])
    f_left[...] = b_dl[...].astype(F32).reshape(1024, 128)
    back(0, f_left)
    arrived(b_dr, recv.at[5])
    f_right[...] = b_dr[...].astype(F32).reshape(1024, 128)
    back(128, f_right)
    along_col(lambda n: s_src.at[n], s_got, send.at[10], recv.at[10], r, c)

    arrived(e_parts, recv.at[9])
    e_tot[...] = jnp.sum(e_parts[...], axis=0)
    along_col(lambda n: e_tot, e_out, send.at[11], recv.at[11], r, c)

    arrived(s_got, recv.at[10])
    s_part[...] = jnp.sum(s_got[...], axis=0)
    along_row(s_part, s_parts, send.at[12], recv.at[12], r, c)

    def last(q, _):
        at = pl.ds(pl.multiple_of(q * 128, 128), 128)
        dx = dot(w_proj[...], dpb[:, at]) + dot(w_gin[...], dgb[:, at]) + dot(w_gout[...], dsb[:, at])
        x_f = xh[q]
        dx = dx - jnp.mean(dx, axis=0, keepdims=True) - x_f * jnp.mean(dx * x_f, axis=0, keepdims=True)
        u = (ctt[q] + rstd[q][:1] * dx).astype(BF)
        gpair[pl.ds(q * 4, 4)] = dot(u, eye, ((0,), (0,))).astype(BF).reshape(4, 32, 128)
        return 0

    lax.fori_loop(0, 8, last, 0)

    arrived(s_parts, recv.at[12])
    s_tot[...] = jnp.sum(s_parts[...], axis=0)
    along_col(lambda n: s_tot, s_out, send.at[13], recv.at[13], r, c)
    scale = 1.0 / 512
    arrived(e_out, recv.at[11])
    g_gout[...] = e_out[pl.ds(0, 8)].reshape(128, 128) * scale
    g_out[...] = e_out[pl.ds(8, 8)].reshape(128, 128) * scale
    arrived(s_out, recv.at[13])
    for lo in (0, 128):
        n = lo // 32
        g_proj[:, lo:lo + 128] = s_out[pl.ds(n, 4)].reshape(128, 128) * scale
        g_gin[:, lo:lo + 128] = s_out[pl.ds(8 + n, 4)].reshape(128, 128) * scale

    for n in range(6):
        sent(m_r, send.at[n], r, c)
    swap.wait_send()
    cross.wait_send()
    for n in (7, 9, 11):
        arrived(e_got.at[pl.ds(0, 15)], send.at[n])
    for n in (10, 12, 13):
        arrived(s_got.at[pl.ds(0, 15)], send.at[n])


def shards(pair, cotangent, chain_counts, crop_skip, w_proj, w_gate_in, w_gate_out, w_out):
    vmem = pl.BlockSpec(memory_space=pltpu.VMEM)
    smem = pl.BlockSpec(memory_space=pltpu.SMEM)
    v = pltpu.VMEM
    scratch = (
        [v((256, 128), BF), v((256, 128), BF), v((128, 128), BF), v((128, 128), BF), v((512, 512), BF)]
        + [v((8, 128, 128), F32), v((128, 1024), BF), v((8, 8, 128), F32), v((8, 128, 128), F32), v((8, 128, 128), F32)]
        + [v((8, 256, 128), F32), v((8, 256, 128), F32)]
        + [v((8, 128, 128), F32)] * 3
        + [v((128, 1024), BF)] * 3
        + [v((256, 1024), BF)] * 2
        + [v((1024, 128), F32)] * 2
        + [v((1024, 128), F32), v((256, 512), BF), v((512, 512), BF), v((256, 512), BF)]
        + [v((256, 512), F32)] * 2
        + [v((128, 8, 128), BF)] * 2 + [v((8, 16, 8, 128), BF)] + [v((128, 8, 128), BF)] + [v((8, 16, 8, 128), BF)] * 2
        + [v((8, 16, 8, 128), BF)] * 2 + [v((128, 8, 128), BF)] + [v((8, 16, 8, 128), BF)] + [v((128, 8, 128), BF)] * 2
        + [v((16, 16, 128), F32)] * 2 + [v((16, 128), F32), v((16, 16, 128), F32), v((16, 128), F32), v((16, 16, 128), F32)]
        + [v((16, 32, 128), F32)] * 2 + [v((32, 128), F32), v((16, 32, 128), F32), v((32, 128), F32), v((16, 32, 128), F32)]
        + [pltpu.SemaphoreType.DMA((14,)), pltpu.SemaphoreType.DMA((14,)), pltpu.SemaphoreType.REGULAR((1,))]
    )
    s = jax.ShapeDtypeStruct
    return pl.pallas_call(
        kernel,
        out_shape=(
            s((32, 32, 128), BF), s((32, 32, 128), BF), s((128, 256), F32), s((128, 256), F32),
            s((128, 128), F32), s((128, 128), F32),
        ),
        in_specs=[smem, smem] + [vmem] * 6,
        out_specs=(vmem,) * 6,
        scratch_shapes=scratch,
        compiler_params=pltpu.CompilerParams(collective_id=1, has_side_effects=True, vmem_limit_bytes=48 << 20),
    )(chain_counts, crop_skip, pair, cotangent, w_proj, w_gate_in, w_gate_out, w_out)


def solution(mesh):
    in_specs = (P("row", "col", None), P("row", "col", None), P(), P(), P(), P(), P(), P())
    out_specs = (P("row", "col", None), P("row", "col", None), P(), P(), P(), P())
    return jax.shard_map(shards, mesh=mesh, in_specs=in_specs, out_specs=out_specs, check_vma=False)
```

time: 1080 us -> 110 us (0.10)
  waiting for transfers between devices: 963 us -> 0 us
  Pallas kernels: 0 us -> 98.3 us
  local copies, waits for them, and re-layouts: 56.6 us -> 10.4 us
  matrix products: 26.5 us -> 0 us
  other arithmetic: 20.5 us -> 0 us
  between operations: 14.1 us -> 0.66 us
    psum x3 -> x0, waiting for transfers between devices: 570 us -> none  [the longest x2 320 us: from_root(): return lax.psum(jnp.where(mine, array, jnp.zeros_like(array)), axis)]
    all_gather x6 -> x0, waiting for transfers between devices: 390 us -> none  [the longest x1 97 us: shards(): grad_slab = lax.all_gather(d_tri, 'row', axis=0, tiled=True)]
    pallas_call x0 -> x1, Pallas kernels: none -> 98.3 us  [shards(): pl.pallas_call(kernel, out_shape=(s((32, 32, 128), BF), s((32, 32, 128),...]
    all_gather x5 -> x0, local copies, waits for them, and re-layouts: 41.6 us -> none  [the longest x1 8.62 us: shards(): lax.all_gather(left, 'row', axis=0, tiled=True)]
    dot_general x15 -> x0, matrix products: 26.5 us -> none  [the longest x1 4.7 us: shards(): jnp.einsum('ikh,jkh->ijh', lax.all_gather(left, 'col', axis=1, tiled=True...]
  transfers between devices with their start and end apart: 9 -> 0, of which waited for: 9 -> 0; matrix products, arithmetic and copies ran while one was open for 5% -> 0% of each run, Pallas kernels for 0% -> 0%
where the time goes in v2:
time: 110 us; the launch traced here: 109 us
  Pallas kernels  98.3 us (89%)
  local copies, waits for them, and re-layouts  10.4 us (9%)
    pallas_call x1, Pallas kernels, shards(): pl.pallas_call(kernel, out_shape=(s((32, 32, 128), BF), s((32, 32, 128),...  98.3 us
    unnamed x22, local copies, waits for them, and re-layouts  10.4 us

profile of v2, /device:TPU:1, one launch (start us, length us, event | category | flops | bytes accessed | tf_op | source)
XLA Modules:
  0.0 109.4 jit_solution(6900815811477447515)
XLA Ops:
  0.6 0.0 copy-start
  0.6 0.9 copy-done
  1.6 0.0 copy-start.1
  1.6 0.9 copy-done.1
  2.5 0.0 copy-start.2
  2.5 0.8 copy-done.2
  3.4 0.0 copy-start.3
  3.4 0.8 copy-done.3
  4.2 0.0 copy-start.4
  4.2 0.8 copy-done.4
  5.0 0.0 copy-start.5
  5.0 0.8 copy-done.5
  5.7 0.0 copy-start.6
  5.7 0.7 copy-done.6
  6.4 0.0 copy-start.7
  6.4 0.7 copy-done.7
  7.0 98.3 %shard_map.127 = (bf16[32,32,128]{2,1,0:T(8,128)(2,1)S(1)}, bf16[32,32,128]{2,1,0:T(8,128)(2,1)S(1)}, f32[128,256]{1,0:T(8,128)S(1)}, f32[128,256]{1,0:T(8,128)S...) custom-call(s32[4]{0:T(128)S(1)} %copy-done.6, s32[4]{0:T(128)S(1)} %copy-done.7, bf16[32,32,128]{2,1,0:T(8,128)(2,1)S(1)} %copy-done, ...), custom_call_target="tpu_custom_call" | custom-call | tf_op jit(solution)/shard_map/pallas_call | solution.py:385
  105.4 0.7 copy.20
  106.1 0.7 copy.21
  106.8 0.7 copy.22
  107.5 0.7 copy.23
  108.1 0.6 copy.24
  108.7 0.6 copy.25
Async XLA Ops:
  0.6 1.0 copy-start
  1.6 0.9 copy-start.1
  2.5 0.8 copy-start.2
  3.4 0.8 copy-start.3
  4.2 0.8 copy-start.4
  5.0 0.8 copy-start.5
  5.7 0.7 copy-start.6
  6.4 0.7 copy-start.7

commit v3 on v2

--- a/solution.py
+++ b/solution.py
@@ -46,6 +46,16 @@
     pltpu.make_async_copy(buf, buf, sem).wait()
 
 
+def far_first(u):
+    y = u >> 2
+    dy = jnp.where(y == 0, 2, jnp.where(y == 1, 1, jnp.where(y == 2, 3, 0)))
+    return 1 - (u & 1), 1 - ((u >> 1) & 1), dy
+
+
+def other_chip(m, dx, dy):
+    return (((m >> 2) ^ dx) << 2) + (((m & 3) + dy) & 3)
+
+
 def to_channels(src, dst, send, recv, r, c):
     half, m, core = r // 8, c // 2, lax.rem(c, 2)
     r8 = lax.rem(r, 8)
@@ -60,12 +70,16 @@
         remote(src.at[own], dst.at[r8, c], send, recv, (r, m * 2 + half)).start()
 
     def body(s, _):
-        r2 = lax.rem(r + lax.rem(s, 16), 16)
-        m2 = lax.rem(m + s // 16, 8)
+        dxh, dxl, dy = far_first(s >> 3)
+        t = s & 7
+        k = (t + 1) >> 1
+        z = ((r >> 1) + jnp.where((t & 1) == 1, 4 - k, 4 + k)) & 7
+        r2 = z * 2 + ((r & 1) ^ dxh)
+        m2 = other_chip(m, dxl, dy)
         remote(src.at[r2 * 8 + m2], dst.at[r8, c], send, recv, (r2, m2 * 2 + half)).start()
         return 0
 
-    lax.fori_loop(1, 128, body, 0)
+    lax.fori_loop(0, 127, body, 0)
 
 
 def to_cells(src, dst, send, recv, r, c):
@@ -82,12 +96,14 @@
         remote(src.at[r8, c], dst.at[channel], send, recv, (core * 8 + r8, c)).start()
 
     def body(s, _):
-        q = lax.rem(r + lax.rem(s, 8), 8)
-        c2 = lax.rem(c + s // 8, 16)
+        dxh, dxl, dy = far_first(s >> 3)
+        z = ((r >> 1) + 1 + s) & 3
+        q = z * 2 + ((r & 1) ^ dxh)
+        c2 = other_chip(m, dxl, dy) * 2 + (core ^ 1 ^ ((s >> 2) & 1))
         remote(src.at[q, c2], dst.at[channel], send, recv, (core * 8 + q, c2)).start()
         return 0
 
-    lax.fori_loop(1, 128, body, 0)
+    lax.fori_loop(0, 127, body, 0)
 
 
 def sent(src, send, r, c):
@@ -135,33 +151,42 @@
 
 
 def kernel(
-    counts, skip, pair, cot, w_proj, w_gin, w_gout, w_out,
-    upd, gpair, g_proj, g_gin, g_gout, g_out,
+    counts_h, skip_h, pair_h, cot_h, w_proj_h, w_gin_h, w_gout_h, w_out_h,
+    upd_h, gpair_h, sums_h,
+    counts, skip, pair, cot, w_proj, w_gin, w_gout, w_out, upd, gpair,
     wp_t, wg_t, wgo_t, wo_t, perm,
     xh, xb, rstd, pt, ctt, gate, slope, go, dgo, dtn, dyb, tnb, dsb, dpb, dgb,
     f_left, f_right, f_mat, left, right, dmat, partial, got,
     m_r, m_l, m_t, m_d, m_dl, m_dr,
     b_r, b_l, b_t, b_d, b_dl, b_dr,
-    e_src, e_got, e_part, e_parts, e_tot, e_out,
     s_src, s_got, s_part, s_parts, s_tot, s_out,
-    send, recv, reg,
+    send, recv, load, reg,
 ):
+    pending = []
+
     r, c = lax.axis_index("row"), lax.axis_index("col")
     core = lax.rem(c, 2)
     sibling = (r, c + 1 - 2 * core)
     greet(r, c)
-
-    wp_t[...] = w_proj[...].astype(F32).T.astype(BF)
-    wg_t[...] = w_gin[...].astype(F32).T.astype(BF)
-    wgo_t[...] = w_gout[...].astype(F32).T.astype(BF)
-    wo_t[...] = w_out[...].astype(F32).T.astype(BF)
+    loads = [
+        pltpu.make_async_copy(a, b, load.at[n])
+        for n, (a, b) in enumerate([
+            (pair_h, pair), (w_proj_h, w_proj), (w_gin_h, w_gin), (counts_h, counts), (skip_h, skip),
+            (cot_h, cot), (w_gout_h, w_gout), (w_out_h, w_out),
+        ])
+    ]
+    for copy in loads:
+        copy.start()
     i0 = lax.broadcasted_iota(jnp.int32, (128, 128), 0)
     i1 = lax.broadcasted_iota(jnp.int32, (128, 128), 1)
     eye = jnp.where(i0 == i1, 1.0, 0.0).astype(BF)
-
+    for copy in loads[:5]:
+        copy.wait()
+    wp_t[...] = w_proj[...].astype(F32).T.astype(BF)
+    wg_t[...] = w_gin[...].astype(F32).T.astype(BF)
     tell(r, c, reg.at[0])
 
-    def forward(q, _):
+    def normed(q, _):
         p = pair[pl.ds(q * 4, 4)].reshape(128, 128)
         p_t = dot(eye, p, ((1,), (1,)))
         pt[q] = p_t
@@ -170,34 +195,46 @@
         var = jnp.mean(dev * dev, axis=0, keepdims=True)
         rs = 1.0 / jnp.sqrt(var + EPS)
         x_f = dev * rs
-        x = x_f.astype(BF)
         xh[q] = x_f
         rstd[q] = jnp.broadcast_to(rs, (8, 128))
-        at = pl.ds(pl.multiple_of(q * 128, 128), 128)
-        xb[:, at] = x
-        s = dot(wp_t[...], x)
-        sig = jax.nn.sigmoid(dot(wg_t[...], x))
-        lane = lax.broadcasted_iota(jnp.int32, (1, 128), 1)
-        mask = valid_of(r * 32 + q * 4 + lane // 32, counts, skip) * valid_of(c * 32 + lane % 32, counts, skip)
-        open_ = mask * sig
-        both = open_ * s
-        gate[q] = open_
-        slope[q] = both * (1.0 - sig)
-        f_left[pl.ds(q, 128, stride=8), :] = both[:128]
-        f_right[pl.ds(q, 128, stride=8), :] = both[128:]
-        return 0
-
-    lax.fori_loop(0, 8, forward, 0)
+        xb[:, pl.ds(pl.multiple_of(q * 128, 128), 128)] = x_f.astype(BF)
+        return 0
+
+    def project(lo, f):
+        def body(q, _):
+            x = xb[:, pl.ds(pl.multiple_of(q * 128, 128), 128)]
+            s = dot(wp_t[lo:lo + 128, :], x)
+            sig = jax.nn.sigmoid(dot(wg_t[lo:lo + 128, :], x))
+            lane = lax.broadcasted_iota(jnp.int32, (1, 128), 1)
+            mask = valid_of(r * 32 + q * 4 + lane // 32, counts, skip) * valid_of(c * 32 + lane % 32, counts, skip)
+            open_ = mask * sig
+            both = open_ * s
+            gate[q, lo:lo + 128] = open_
+            slope[q, lo:lo + 128] = both * (1.0 - sig)
+            f[pl.ds(q, 128, stride=8), :] = both
+            return 0
+
+        lax.fori_loop(0, 8, body, 0)
+
+    lax.fori_loop(0, 8, normed, 0)
+    project(128, f_right)
     m_r[...] = f_right[...].reshape(128, 8, 128).astype(BF)
     pl.semaphore_wait(reg.at[0], 15)
     to_channels(m_r, b_r, send.at[0], recv.at[0], r, c)
+    pending.append(lambda: sent(m_r, send.at[0], r, c))
+    project(0, f_left)
     m_l[...] = f_left[...].reshape(128, 8, 128).astype(BF)
     to_channels(m_l, b_l, send.at[1], recv.at[1], r, c)
+    pending.append(lambda: sent(m_r, send.at[1], r, c))
 
     j0 = lax.broadcasted_iota(jnp.int32, (512, 512), 0)
     j1 = lax.broadcasted_iota(jnp.int32, (512, 512), 1)
     swapped = (j0 % 128) // 32 * 128 + j0 // 128 * 32 + j0 % 32
     perm[...] = jnp.where(swapped == j1, 1.0, 0.0).astype(BF)
+    for copy in loads[5:]:
+        copy.wait()
+    wgo_t[...] = w_gout[...].astype(F32).T.astype(BF)
+    wo_t[...] = w_out[...].astype(F32).T.astype(BF)
 
     def before(q, _):
         at = pl.ds(pl.multiple_of(q * 128, 128), 128)
@@ -239,16 +276,41 @@
             for n in range(4):
                 out[:, 4 * g + n] = o[g * 64:(g + 1) * 64, n * 128:(n + 1) * 128].reshape(8, 8, 128).astype(BF)
 
+    def scatter(n):
+        along_col(lambda k: s_src.at[n, k], s_got.at[n], send.at[8 + n], recv.at[8 + n], r, c)
+        pending.append(lambda: arrived(s_got.at[n, pl.ds(0, 15)], send.at[8 + n]))
+
+    def share(n):
+        arrived(s_got.at[n], recv.at[8 + n])
+        s_part[n] = jnp.sum(s_got[n], axis=0).astype(BF)
+        along_row(s_part.at[n], s_parts.at[n], send.at[11 + n], recv.at[11 + n], r, c)
+        pending.append(lambda: arrived(s_parts.at[n, pl.ds(0, 15)], send.at[11 + n]))
+
+    def gather(n):
+        arrived(s_parts.at[n], recv.at[11 + n])
+        s_tot[n] = jnp.sum(s_parts[n].astype(F32), axis=0) * (1.0 / 512)
+        along_col(lambda k: s_tot.at[n], s_out.at[n], send.at[14 + n], recv.at[14 + n], r, c)
+        pending.append(lambda: arrived(s_got.at[n, pl.ds(0, 15)], send.at[14 + n]))
+
+    outs = []
+
+    def put(src, dst, n):
+        copy = pltpu.make_async_copy(src, dst, load.at[8 + n])
+        copy.start()
+        outs.append(copy)
+
+    mine = right.at[pl.ds(pl.multiple_of(core * 256, 256), 256)]
     arrived(b_r, recv.at[0])
-    mine = right.at[pl.ds(pl.multiple_of(core * 256, 256), 256)]
     matrix(b_r, mine)
     swap = remote(mine, mine, send.at[6], recv.at[6], sibling)
     swap.start()
+    pending.append(swap.wait_send)
     arrived(b_l, recv.at[1])
     matrix(b_l, left)
     swap.wait_recv()
     messages(dot(left[...], right[...], ((1,), (1,))), m_t)
     to_cells(m_t, b_t, send.at[2], recv.at[2], r, c)
+    pending.append(lambda: sent(m_r, send.at[2], r, c))
     arrived(b_t, recv.at[2])
     f_left[...] = b_t[...].astype(F32).reshape(1024, 128)
 
@@ -266,6 +328,7 @@
     lax.fori_loop(0, 8, middle, 0)
     m_d[...] = f_right[...].reshape(128, 8, 128).astype(BF)
     to_channels(m_d, b_d, send.at[3], recv.at[3], r, c)
+    pending.append(lambda: sent(m_r, send.at[3], r, c))
 
     def after(q, _):
         at = pl.ds(pl.multiple_of(q * 128, 128), 128)
@@ -276,29 +339,30 @@
         return 0
 
     lax.fori_loop(0, 8, after, 0)
-    e_src[pl.ds(0, 8)] = dot(xb[...], dsb[...], ((1,), (1,))).reshape(8, 16, 128)
-    e_src[pl.ds(8, 8)] = dot(tnb[...], dyb[...], ((1,), (1,))).reshape(8, 16, 128)
-    along_col(lambda n: e_src.at[n], e_got, send.at[7], recv.at[7], r, c)
+    put(upd, upd_h, 0)
+    s_src[0, pl.ds(0, 8)] = dot(xb[...], dsb[...], ((1,), (1,))).reshape(8, 16, 128)
+    s_src[0, pl.ds(8, 8)] = dot(tnb[...], dyb[...], ((1,), (1,))).reshape(8, 16, 128)
+    scatter(0)
 
     arrived(b_d, recv.at[3])
     matrix(b_d, dmat)
     theirs = pl.ds(pl.multiple_of((1 - core) * 256, 256), 256)
     ours = pl.ds(pl.multiple_of(core * 256, 256), 256)
     partial[...] = dot(dmat[:, theirs], left[...], ((0,), (0,)))
-    cross = remote(partial, got, send.at[8], recv.at[8], sibling)
+    cross = remote(partial, got, send.at[7], recv.at[7], sibling)
     cross.start()
+    pending.append(cross.wait_send)
     messages(dot(dmat[...], right[...]), m_dl)
     to_cells(m_dl, b_dl, send.at[4], recv.at[4], r, c)
+    pending.append(lambda: sent(m_r, send.at[4], r, c))
     part = dot(dmat[:, ours], left[...], ((0,), (0,)))
     cross.wait_recv()
     messages(part + got[...], m_dr)
     to_cells(m_dr, b_dr, send.at[5], recv.at[5], r, c)
-
-    arrived(e_got, recv.at[7])
-    e_part[...] = jnp.sum(e_got[...], axis=0)
-    along_row(e_part, e_parts, send.at[9], recv.at[9], r, c)
-
-    def back(lo, f):
+    pending.append(lambda: sent(m_r, send.at[5], r, c))
+    share(0)
+
+    def back(n, lo, f):
         def body(q, _):
             at = pl.ds(pl.multiple_of(q * 128, 128), 128)
             d = f[pl.ds(q, 128, stride=8), :]
@@ -307,25 +371,19 @@
             return 0
 
         lax.fori_loop(0, 8, body, 0)
-        n = lo // 32
-        s_src[pl.ds(n, 4)] = dot(xb[...], dpb[lo:lo + 128, :], ((1,), (1,))).reshape(4, 32, 128)
-        s_src[pl.ds(8 + n, 4)] = dot(xb[...], dgb[lo:lo + 128, :], ((1,), (1,))).reshape(4, 32, 128)
+        s_src[n, pl.ds(0, 8)] = dot(xb[...], dpb[lo:lo + 128, :], ((1,), (1,))).reshape(8, 16, 128)
+        s_src[n, pl.ds(8, 8)] = dot(xb[...], dgb[lo:lo + 128, :], ((1,), (1,))).reshape(8, 16, 128)
+        scatter(n)
 
     arrived(b_dl, recv.at[4])
     f_left[...] = b_dl[...].astype(F32).reshape(1024, 128)
-    back(0, f_left)
+    back(1, 0, f_left)
+    gather(0)
+    share(1)
     arrived(b_dr, recv.at[5])
     f_right[...] = b_dr[...].astype(F32).reshape(1024, 128)
-    back(128, f_right)
-    along_col(lambda n: s_src.at[n], s_got, send.at[10], recv.at[10], r, c)
-
-    arrived(e_parts, recv.at[9])
-    e_tot[...] = jnp.sum(e_parts[...], axis=0)
-    along_col(lambda n: e_tot, e_out, send.at[11], recv.at[11], r, c)
-
-    arrived(s_got, recv.at[10])
-    s_part[...] = jnp.sum(s_got[...], axis=0)
-    along_row(s_part, s_parts, send.at[12], recv.at[12], r, c)
+    back(2, 128, f_right)
+    gather(1)
 
     def last(q, _):
         at = pl.ds(pl.multiple_of(q * 128, 128), 128)
@@ -336,37 +394,53 @@
         gpair[pl.ds(q * 4, 4)] = dot(u, eye, ((0,), (0,))).astype(BF).reshape(4, 32, 128)
         return 0
 
-    lax.fori_loop(0, 8, last, 0)
-
-    arrived(s_parts, recv.at[12])
-    s_tot[...] = jnp.sum(s_parts[...], axis=0)
-    along_col(lambda n: s_tot, s_out, send.at[13], recv.at[13], r, c)
-    scale = 1.0 / 512
-    arrived(e_out, recv.at[11])
-    g_gout[...] = e_out[pl.ds(0, 8)].reshape(128, 128) * scale
-    g_out[...] = e_out[pl.ds(8, 8)].reshape(128, 128) * scale
-    arrived(s_out, recv.at[13])
-    for lo in (0, 128):
-        n = lo // 32
-        g_proj[:, lo:lo + 128] = s_out[pl.ds(n, 4)].reshape(128, 128) * scale
-        g_gin[:, lo:lo + 128] = s_out[pl.ds(8 + n, 4)].reshape(128, 128) * scale
-
-    for n in range(6):
-        sent(m_r, send.at[n], r, c)
-    swap.wait_send()
-    cross.wait_send()
-    for n in (7, 9, 11):
-        arrived(e_got.at[pl.ds(0, 15)], send.at[n])
-    for n in (10, 12, 13):
-        arrived(s_got.at[pl.ds(0, 15)], send.at[n])
+    lax.fori_loop(0, 4, last, 0)
+    share(2)
+    lax.fori_loop(4, 8, last, 0)
+    put(gpair, gpair_h, 1)
+    for n in range(2):
+        arrived(s_out.at[n], recv.at[14 + n])
+        put(s_out.at[n], sums_h.at[n], 2 + n)
+    gather(2)
+    for wait in pending:
+        wait()
+    arrived(s_out.at[2], recv.at[16])
+    put(s_out.at[2], sums_h.at[2], 4)
+    for copy in outs:
+        copy.wait()
+
+
+def finish(upd, gpair, sums, upd_o, gpair_o, g_proj, g_gin, g_gout, g_out, upd_v, gpair_v, sums_v, sem):
+    loads = [
+        pltpu.make_async_copy(a, b, sem.at[n])
+        for n, (a, b) in enumerate([(upd, upd_v), (gpair, gpair_v), (sums, sums_v)])
+    ]
+    for copy in loads:
+        copy.start()
+    flat = sums_v.reshape(6, 128, 128)
+    left, right = pl.ds(0, 128), pl.ds(128, 128)
+    pairs = [
+        (upd_v, upd_o), (gpair_v, gpair_o), (flat.at[0], g_gout), (flat.at[1], g_out),
+        (flat.at[2], g_proj.at[:, left]), (flat.at[3], g_gin.at[:, left]),
+        (flat.at[4], g_proj.at[:, right]), (flat.at[5], g_gin.at[:, right]),
+    ]
+    stores = [pltpu.make_async_copy(a, b, sem.at[3 + n]) for n, (a, b) in enumerate(pairs)]
+    for n, copy in enumerate(stores):
+        if n < 3:
+            loads[n].wait()
+        copy.start()
+    for copy in stores:
+        copy.wait()
 
 
 def shards(pair, cotangent, chain_counts, crop_skip, w_proj, w_gate_in, w_gate_out, w_out):
-    vmem = pl.BlockSpec(memory_space=pltpu.VMEM)
-    smem = pl.BlockSpec(memory_space=pltpu.SMEM)
+    hbm = pl.BlockSpec(memory_space=pl.ANY)
     v = pltpu.VMEM
+    s = jax.ShapeDtypeStruct
     scratch = (
-        [v((256, 128), BF), v((256, 128), BF), v((128, 128), BF), v((128, 128), BF), v((512, 512), BF)]
+        [pltpu.SMEM((4,), jnp.int32)] * 2 + [v((32, 32, 128), BF)] * 2
+        + [v((128, 256), BF)] * 2 + [v((128, 128), BF)] * 2 + [v((32, 32, 128), BF)] * 2
+        + [v((256, 128), BF), v((256, 128), BF), v((128, 128), BF), v((128, 128), BF), v((512, 512), BF)]
         + [v((8, 128, 128), F32), v((128, 1024), BF), v((8, 8, 128), F32), v((8, 128, 128), F32), v((8, 128, 128), F32)]
         + [v((8, 256, 128), F32), v((8, 256, 128), F32)]
         + [v((8, 128, 128), F32)] * 3
@@ -377,22 +451,29 @@
         + [v((256, 512), F32)] * 2
         + [v((128, 8, 128), BF)] * 2 + [v((8, 16, 8, 128), BF)] + [v((128, 8, 128), BF)] + [v((8, 16, 8, 128), BF)] * 2
         + [v((8, 16, 8, 128), BF)] * 2 + [v((128, 8, 128), BF)] + [v((8, 16, 8, 128), BF)] + [v((128, 8, 128), BF)] * 2
-        + [v((16, 16, 128), F32)] * 2 + [v((16, 128), F32), v((16, 16, 128), F32), v((16, 128), F32), v((16, 16, 128), F32)]
-        + [v((16, 32, 128), F32)] * 2 + [v((32, 128), F32), v((16, 32, 128), F32), v((32, 128), F32), v((16, 32, 128), F32)]
-        + [pltpu.SemaphoreType.DMA((14,)), pltpu.SemaphoreType.DMA((14,)), pltpu.SemaphoreType.REGULAR((1,))]
+        + [v((3, 16, 16, 128), F32)] * 2 + [v((3, 16, 128), BF), v((3, 16, 16, 128), BF), v((3, 16, 128), F32)]
+        + [v((3, 16, 16, 128), F32)]
+        + [pltpu.SemaphoreType.DMA((17,)), pltpu.SemaphoreType.DMA((17,)), pltpu.SemaphoreType.DMA((13,))]
+        + [pltpu.SemaphoreType.REGULAR((1,))]
     )
-    s = jax.ShapeDtypeStruct
+    block = s((32, 32, 128), BF)
+    wide, square = s((128, 256), F32), s((128, 128), F32)
+    results = pl.pallas_call(
+        kernel,
+        out_shape=(block, block, s((3, 16, 16, 128), F32)),
+        in_specs=[hbm] * 8,
+        out_specs=(hbm,) * 3,
+        scratch_shapes=scratch,
+        compiler_params=pltpu.CompilerParams(collective_id=1, has_side_effects=True, vmem_limit_bytes=60 << 20),
+    )(chain_counts, crop_skip, pair, cotangent, w_proj, w_gate_in, w_gate_out, w_out)
     return pl.pallas_call(
-        kernel,
-        out_shape=(
-            s((32, 32, 128), BF), s((32, 32, 128), BF), s((128, 256), F32), s((128, 256), F32),
-            s((128, 128), F32), s((128, 128), F32),
-        ),
-        in_specs=[smem, smem] + [vmem] * 6,
-        out_specs=(vmem,) * 6,
-        scratch_shapes=scratch,
-        compiler_params=pltpu.CompilerParams(collective_id=1, has_side_effects=True, vmem_limit_bytes=48 << 20),
-    )(chain_counts, crop_skip, pair, cotangent, w_proj, w_gate_in, w_gate_out, w_out)
+        finish,
+        out_shape=(block, block, wide, wide, square, square),
+        in_specs=[hbm] * 3,
+        out_specs=(hbm,) * 6,
+        scratch_shapes=[v(block.shape, BF)] * 2 + [v((3, 16, 16, 128), F32), pltpu.SemaphoreType.DMA((11,))],
+        compiler_params=pltpu.CompilerParams(vmem_limit_bytes=60 << 20),
+    )(*results)
 
 
 def solution(mesh):

time: 110 us -> 95.6 us (0.87)
  local copies, waits for them, and re-layouts: 10.4 us -> 0 us
  Pallas kernels: 98.3 us -> 94.9 us
    unnamed x22 -> x0, local copies, waits for them, and re-layouts: 10.4 us -> none
    pallas_call x1 -> x2, Pallas kernels: 98.3 us -> 94.9 us  [the longest x1 92.9 us: shards(): pl.pallas_call(kernel, out_shape=(block, block, s((3, 16, 16, 128), F32))...]
where the time goes in v3:
time: 95.6 us; the launch traced here: 95.5 us
  Pallas kernels  94.9 us (99%)
    pallas_call x1, Pallas kernels, shards(): pl.pallas_call(kernel, out_shape=(block, block, s((3, 16, 16, 128), F32))...  92.9 us
    pallas_call x1, Pallas kernels, shards(): pl.pallas_call(finish, out_shape=(block, block, wide, wide, square, squar...  1.99 us

profile of v3, /device:TPU:1, one launch (start us, length us, event | category | flops | bytes accessed | tf_op | source)
XLA Modules:
  0.0 95.5 jit_solution(16357716488632051140)
XLA Ops:
  0.6 92.9 %shard_map.127 = (bf16[32,32,128]{2,1,0:T(8,128)(2,1)}, bf16[32,32,128]{2,1,0:T(8,128)(2,1)}, f32[3,16,16,128]{3,2,1,0:T(8,128)}) custom-call(s32[4]{0:T(128)} %counts_h.1, s32[4]{0:T(128)} %skip_h.1, bf16[32,32,128]{2,1,0:T(8,128)(2,1)} %pair_h.1, bf16[32,32,128]{2,1,0:T(8,128)(2,1)} %cot_h.1, bf16[128,256]{1,0:T(8,128)(2,1)} %w_proj_h.1, ...), custom_call_target="tpu_custom_call" | custom-call | tf_op jit(solution)/shard_map/pallas_call | solution.py:461
  93.5 2.0 %shard_map.128 = (bf16[32,32,128]{2,1,0:T(8,128)(2,1)}, bf16[32,32,128]{2,1,0:T(8,128)(2,1)}, f32[128,256]{1,0:T(8,128)}, f32[128,256]{1,0:T(8,128)}, f32[128,128]{1,0:T(8,128)}, /*index=5*/f32[128,128]{1,0:T(8,128)}) custom-call(bf16[32,32,128]{2,1,0:T(8,128)(2,1)} %get-tuple-element.9.upd, bf16[32,32,128]{2,1,0:T(8,128)(2,1)} %get-tuple-element.10.gpair, ...), custom_call_target="tpu_custom_call" | custom-call | tf_op jit(solution)/shard_map/pallas_call | solution.py:469

commit v4 on v3

--- a/solution.py
+++ b/solution.py
@@ -159,7 +159,7 @@
     f_left, f_right, f_mat, left, right, dmat, partial, got,
     m_r, m_l, m_t, m_d, m_dl, m_dr,
     b_r, b_l, b_t, b_d, b_dl, b_dr,
-    s_src, s_got, s_part, s_parts, s_tot, s_out,
+    s_src, s_got, s_part, s_parts, s_tot, s_out, s_sum,
     send, recv, load, reg,
 ):
     pending = []
@@ -180,6 +180,10 @@
     i0 = lax.broadcasted_iota(jnp.int32, (128, 128), 0)
     i1 = lax.broadcasted_iota(jnp.int32, (128, 128), 1)
     eye = jnp.where(i0 == i1, 1.0, 0.0).astype(BF)
+    j0 = lax.broadcasted_iota(jnp.int32, (512, 512), 0)
+    j1 = lax.broadcasted_iota(jnp.int32, (512, 512), 1)
+    swapped = ((j0 >> 5) & 3) * 128 + (j0 >> 7) * 32 + (j0 & 31)
+    perm[...] = jnp.where(swapped == j1, 1.0, 0.0).astype(BF)
     for copy in loads[:5]:
         copy.wait()
     wp_t[...] = w_proj[...].astype(F32).T.astype(BF)
@@ -214,9 +218,9 @@
             f[pl.ds(q, 128, stride=8), :] = both
             return 0
 
-        lax.fori_loop(0, 8, body, 0)
-
-    lax.fori_loop(0, 8, normed, 0)
+        lax.fori_loop(0, 8, body, 0, unroll=4)
+
+    lax.fori_loop(0, 8, normed, 0, unroll=4)
     project(128, f_right)
     m_r[...] = f_right[...].reshape(128, 8, 128).astype(BF)
     pl.semaphore_wait(reg.at[0], 15)
@@ -226,15 +230,6 @@
     m_l[...] = f_left[...].reshape(128, 8, 128).astype(BF)
     to_channels(m_l, b_l, send.at[1], recv.at[1], r, c)
     pending.append(lambda: sent(m_r, send.at[1], r, c))
-
-    j0 = lax.broadcasted_iota(jnp.int32, (512, 512), 0)
-    j1 = lax.broadcasted_iota(jnp.int32, (512, 512), 1)
-    swapped = (j0 % 128) // 32 * 128 + j0 // 128 * 32 + j0 % 32
-    perm[...] = jnp.where(swapped == j1, 1.0, 0.0).astype(BF)
-    for copy in loads[5:]:
-        copy.wait()
-    wgo_t[...] = w_gout[...].astype(F32).T.astype(BF)
-    wo_t[...] = w_out[...].astype(F32).T.astype(BF)
 
     def before(q, _):
         at = pl.ds(pl.multiple_of(q * 128, 128), 128)
@@ -250,31 +245,42 @@
         dtn[q] = dt - jnp.mean(dt, axis=0, keepdims=True)
         return 0
 
-    lax.fori_loop(0, 8, before, 0)
-
-    def matrix(buf, out):
+
+    def turned(buf):
         rows = []
         for g in range(4):
             cols = [buf[:, 4 * g + n].astype(F32).reshape(64, 128).astype(BF) for n in range(4)]
             rows.append(jnp.concatenate(cols, axis=1))
-        o = dot(jnp.concatenate(rows, axis=0), perm[...])
+        return dot(jnp.concatenate(rows, axis=0), perm[...])
+
+    def natural(buf, out):
+        o = turned(buf)
         for g in range(4):
             for a in range(4):
                 f_mat[pl.ds(g * 256 + a, 64, stride=4), :] = o[g * 64:(g + 1) * 64, a * 128:(a + 1) * 128]
         for g in range(4):
             out[:, g * 128:(g + 1) * 128] = f_mat[g * 256:(g + 1) * 256].astype(BF)
 
-    def messages(mat, out):
-        for g in range(4):
-            f_mat[g * 256:(g + 1) * 256] = mat[:, g * 128:(g + 1) * 128]
-        rows = []
-        for g in range(4):
-            cols = [f_mat[pl.ds(g * 256 + a, 64, stride=4), :].astype(BF) for a in range(4)]
-            rows.append(jnp.concatenate(cols, axis=1))
+    def matrix(buf, out):
+        o = turned(buf)
+        for g in range(4):
+            for a in range(4):
+                out[a * 64:(a + 1) * 64, g * 128:(g + 1) * 128] = o[g * 64:(g + 1) * 64, a * 128:(a + 1) * 128].astype(BF)
+
+    def spread(block, out):
+        rows = [jnp.concatenate([block(a, g).astype(BF) for a in range(4)], axis=1) for g in range(4)]
         o = dot(jnp.concatenate(rows, axis=0), perm[...])
         for g in range(4):
             for n in range(4):
                 out[:, 4 * g + n] = o[g * 64:(g + 1) * 64, n * 128:(n + 1) * 128].reshape(8, 8, 128).astype(BF)
+
+    def messages(mat, out):
+        spread(lambda a, g: mat[a * 64:(a + 1) * 64, g * 128:(g + 1) * 128], out)
+
+    def natural_messages(mat, out):
+        for g in range(4):
+            f_mat[g * 256:(g + 1) * 256] = mat[:, g * 128:(g + 1) * 128]
+        spread(lambda a, g: f_mat[pl.ds(g * 256 + a, 64, stride=4), :], out)
 
     def scatter(n):
         along_col(lambda k: s_src.at[n, k], s_got.at[n], send.at[8 + n], recv.at[8 + n], r, c)
@@ -282,13 +288,13 @@
 
     def share(n):
         arrived(s_got.at[n], recv.at[8 + n])
-        s_part[n] = jnp.sum(s_got[n], axis=0).astype(BF)
+        s_part[n] = jnp.sum(s_got[n].astype(F32), axis=0).astype(BF)
         along_row(s_part.at[n], s_parts.at[n], send.at[11 + n], recv.at[11 + n], r, c)
         pending.append(lambda: arrived(s_parts.at[n, pl.ds(0, 15)], send.at[11 + n]))
 
     def gather(n):
         arrived(s_parts.at[n], recv.at[11 + n])
-        s_tot[n] = jnp.sum(s_parts[n].astype(F32), axis=0) * (1.0 / 512)
+        s_tot[n] = (jnp.sum(s_parts[n].astype(F32), axis=0) * (1.0 / 512)).astype(BF)
         along_col(lambda k: s_tot.at[n], s_out.at[n], send.at[14 + n], recv.at[14 + n], r, c)
         pending.append(lambda: arrived(s_got.at[n, pl.ds(0, 15)], send.at[14 + n]))
 
@@ -301,10 +307,16 @@
 
     mine = right.at[pl.ds(pl.multiple_of(core * 256, 256), 256)]
     arrived(b_r, recv.at[0])
-    matrix(b_r, mine)
+    natural(b_r, mine)
     swap = remote(mine, mine, send.at[6], recv.at[6], sibling)
     swap.start()
     pending.append(swap.wait_send)
+
+    for copy in loads[5:]:
+        copy.wait()
+    wgo_t[...] = w_gout[...].astype(F32).T.astype(BF)
+    wo_t[...] = w_out[...].astype(F32).T.astype(BF)
+    lax.fori_loop(0, 8, before, 0, unroll=2)
     arrived(b_l, recv.at[1])
     matrix(b_l, left)
     swap.wait_recv()
@@ -325,7 +337,7 @@
         f_right[pl.ds(q, 128, stride=8), :] = rs * (d - that * jnp.mean(d * that, axis=0, keepdims=True))
         return 0
 
-    lax.fori_loop(0, 8, middle, 0)
+    lax.fori_loop(0, 8, middle, 0, unroll=4)
     m_d[...] = f_right[...].reshape(128, 8, 128).astype(BF)
     to_channels(m_d, b_d, send.at[3], recv.at[3], r, c)
     pending.append(lambda: sent(m_r, send.at[3], r, c))
@@ -338,17 +350,17 @@
         upd[pl.ds(q * 4, 4)] = dot(u, eye, ((0,), (0,))).astype(BF).reshape(4, 32, 128)
         return 0
 
-    lax.fori_loop(0, 8, after, 0)
+    lax.fori_loop(0, 8, after, 0, unroll=2)
     put(upd, upd_h, 0)
-    s_src[0, pl.ds(0, 8)] = dot(xb[...], dsb[...], ((1,), (1,))).reshape(8, 16, 128)
-    s_src[0, pl.ds(8, 8)] = dot(tnb[...], dyb[...], ((1,), (1,))).reshape(8, 16, 128)
+    s_src[0, pl.ds(0, 8)] = dot(xb[...], dsb[...], ((1,), (1,))).reshape(8, 16, 128).astype(BF)
+    s_src[0, pl.ds(8, 8)] = dot(tnb[...], dyb[...], ((1,), (1,))).reshape(8, 16, 128).astype(BF)
     scatter(0)
 
     arrived(b_d, recv.at[3])
     matrix(b_d, dmat)
     theirs = pl.ds(pl.multiple_of((1 - core) * 256, 256), 256)
     ours = pl.ds(pl.multiple_of(core * 256, 256), 256)
-    partial[...] = dot(dmat[:, theirs], left[...], ((0,), (0,)))
+    partial[...] = dot(dmat[:, theirs], left[...], ((0,), (0,))).astype(BF)
     cross = remote(partial, got, send.at[7], recv.at[7], sibling)
     cross.start()
     pending.append(cross.wait_send)
@@ -356,11 +368,11 @@
     to_cells(m_dl, b_dl, send.at[4], recv.at[4], r, c)
     pending.append(lambda: sent(m_r, send.at[4], r, c))
     part = dot(dmat[:, ours], left[...], ((0,), (0,)))
+    share(0)
     cross.wait_recv()
-    messages(part + got[...], m_dr)
+    natural_messages(part + got[...].astype(F32), m_dr)
     to_cells(m_dr, b_dr, send.at[5], recv.at[5], r, c)
     pending.append(lambda: sent(m_r, send.at[5], r, c))
-    share(0)
 
     def back(n, lo, f):
         def body(q, _):
@@ -370,20 +382,19 @@
             dgb[lo:lo + 128, at] = (d * slope[q, lo:lo + 128]).astype(BF)
             return 0
 
-        lax.fori_loop(0, 8, body, 0)
-        s_src[n, pl.ds(0, 8)] = dot(xb[...], dpb[lo:lo + 128, :], ((1,), (1,))).reshape(8, 16, 128)
-        s_src[n, pl.ds(8, 8)] = dot(xb[...], dgb[lo:lo + 128, :], ((1,), (1,))).reshape(8, 16, 128)
+        lax.fori_loop(0, 8, body, 0, unroll=4)
+        s_src[n, pl.ds(0, 8)] = dot(xb[...], dpb[lo:lo + 128, :], ((1,), (1,))).reshape(8, 16, 128).astype(BF)
+        s_src[n, pl.ds(8, 8)] = dot(xb[...], dgb[lo:lo + 128, :], ((1,), (1,))).reshape(8, 16, 128).astype(BF)
         scatter(n)
 
     arrived(b_dl, recv.at[4])
     f_left[...] = b_dl[...].astype(F32).reshape(1024, 128)
     back(1, 0, f_left)
     gather(0)
-    share(1)
     arrived(b_dr, recv.at[5])
     f_right[...] = b_dr[...].astype(F32).reshape(1024, 128)
     back(2, 128, f_right)
-    gather(1)
+    share(1)
 
     def last(q, _):
         at = pl.ds(pl.multiple_of(q * 128, 128), 128)
@@ -394,18 +405,23 @@
         gpair[pl.ds(q * 4, 4)] = dot(u, eye, ((0,), (0,))).astype(BF).reshape(4, 32, 128)
         return 0
 
-    lax.fori_loop(0, 4, last, 0)
+    lax.fori_loop(0, 4, last, 0, unroll=2)
     share(2)
-    lax.fori_loop(4, 8, last, 0)
+    gather(1)
+    lax.fori_loop(4, 8, last, 0, unroll=2)
     put(gpair, gpair_h, 1)
-    for n in range(2):
+
+    def total(n):
         arrived(s_out.at[n], recv.at[14 + n])
-        put(s_out.at[n], sums_h.at[n], 2 + n)
+        s_sum[n] = s_out[n].astype(F32)
+        put(s_sum.at[n], sums_h.at[n], 2 + n)
+
+    total(0)
     gather(2)
+    total(1)
     for wait in pending:
         wait()
-    arrived(s_out.at[2], recv.at[16])
-    put(s_out.at[2], sums_h.at[2], 4)
+    total(2)
     for copy in outs:
         copy.wait()
 
@@ -448,11 +464,11 @@
         + [v((256, 1024), BF)] * 2
         + [v((1024, 128), F32)] * 2
         + [v((1024, 128), F32), v((256, 512), BF), v((512, 512), BF), v((256, 512), BF)]
-        + [v((256, 512), F32)] * 2
+        + [v((256, 512), BF)] * 2
         + [v((128, 8, 128), BF)] * 2 + [v((8, 16, 8, 128), BF)] + [v((128, 8, 128), BF)] + [v((8, 16, 8, 128), BF)] * 2
         + [v((8, 16, 8, 128), BF)] * 2 + [v((128, 8, 128), BF)] + [v((8, 16, 8, 128), BF)] + [v((128, 8, 128), BF)] * 2
-        + [v((3, 16, 16, 128), F32)] * 2 + [v((3, 16, 128), BF), v((3, 16, 16, 128), BF), v((3, 16, 128), F32)]
-        + [v((3, 16, 16, 128), F32)]
+        + [v((3, 16, 16, 128), BF)] * 2 + [v((3, 16, 128), BF), v((3, 16, 16, 128), BF), v((3, 16, 128), BF)]
+        + [v((3, 16, 16, 128), BF), v((3, 16, 16, 128), F32)]
         + [pltpu.SemaphoreType.DMA((17,)), pltpu.SemaphoreType.DMA((17,)), pltpu.SemaphoreType.DMA((13,))]
         + [pltpu.SemaphoreType.REGULAR((1,))]
     )

time: 95.6 us -> 88.1 us (0.922)
  Pallas kernels: 94.9 us -> 87.3 us
    pallas_call x1, Pallas kernels: 92.9 us -> 85.3 us  [shards(): pl.pallas_call(kernel, out_shape=(block, block, s((3, 16, 16, 128), F32))...]
where the time goes in v4:
time: 88.1 us; the launch traced here: 88 us
  Pallas kernels  87.3 us (99%)
    pallas_call x1, Pallas kernels, shards(): pl.pallas_call(kernel, out_shape=(block, block, s((3, 16, 16, 128), F32))...  85.3 us
    pallas_call x1, Pallas kernels, shards(): pl.pallas_call(finish, out_shape=(block, block, wide, wide, square, squar...  1.99 us

profile of v4, /device:TPU:1, one launch (start us, length us, event | category | flops | bytes accessed | tf_op | source)
XLA Modules:
  0.0 88.0 jit_solution(14049868077470699002)
XLA Ops:
  0.6 85.3 %shard_map.127 = (bf16[32,32,128]{2,1,0:T(8,128)(2,1)}, bf16[32,32,128]{2,1,0:T(8,128)(2,1)}, f32[3,16,16,128]{3,2,1,0:T(8,128)}) custom-call(s32[4]{0:T(128)} %counts_h.1, s32[4]{0:T(128)} %skip_h.1, bf16[32,32,128]{2,1,0:T(8,128)(2,1)} %pair_h.1, bf16[32,32,128]{2,1,0:T(8,128)(2,1)} %cot_h.1, bf16[128,256]{1,0:T(8,128)(2,1)} %w_proj_h.1, ...), custom_call_target="tpu_custom_call" | custom-call | tf_op jit(solution)/shard_map/pallas_call | solution.py:477
  86.0 2.0 %shard_map.128 = (bf16[32,32,128]{2,1,0:T(8,128)(2,1)}, bf16[32,32,128]{2,1,0:T(8,128)(2,1)}, f32[128,256]{1,0:T(8,128)}, f32[128,256]{1,0:T(8,128)}, f32[128,128]{1,0:T(8,128)}, /*index=5*/f32[128,128]{1,0:T(8,128)}) custom-call(bf16[32,32,128]{2,1,0:T(8,128)(2,1)} %get-tuple-element.9.upd, bf16[32,32,128]{2,1,0:T(8,128)(2,1)} %get-tuple-element.10.gpair, ...), custom_call_target="tpu_custom_call" | custom-call | tf_op jit(solution)/shard_map/pallas_call | solution.py:485

commit v5 on v4

v5 whole, which is shorter than its diff:
```python
import jax
import jax.numpy as jnp
from jax import lax
from jax.experimental import pallas as pl
from jax.experimental.pallas import tpu as pltpu
from jax.sharding import PartitionSpec as P

MESH = pl.DeviceIdType.MESH
BF = jnp.bfloat16
F32 = jnp.float32
EPS = 1e-05


def dot(a, b, dims=((1,), (0,))):
    return lax.dot_general(a, b, (dims, ((), ())), preferred_element_type=F32)


def greet(r, c):
    barrier = pltpu.get_barrier_semaphore()
    half, m, core = r // 8, c // 2, lax.rem(c, 2)

    def body(s, _):
        dxh, dxl, dy = far_first(s >> 3)
        z = ((r >> 1) + 1 + s) & 3
        c2 = other_chip(m, dxl, dy) * 2 + (core ^ 1 ^ ((s >> 2) & 1))
        device = (core * 8 + z * 2 + ((r & 1) ^ dxh), c2)
        pl.semaphore_signal(barrier, inc=1, device_id=device, device_id_type=MESH)
        return 0

    lax.fori_loop(0, 127, body, 0)

    @pl.when(core != half)
    def _():
        pl.semaphore_signal(barrier, inc=1, device_id=(core * 8 + lax.rem(r, 8), c), device_id_type=MESH)


def greeted(r, c):
    barrier = pltpu.get_barrier_semaphore()
    same = r // 8 == lax.rem(c, 2)

    @pl.when(same)
    def _():
        pl.semaphore_wait(barrier, 127)

    @pl.when(jnp.logical_not(same))
    def _():
        pl.semaphore_wait(barrier, 128)


def remote(src, dst, send, recv, device):
    return pltpu.make_async_remote_copy(
        src_ref=src, dst_ref=dst, send_sem=send, recv_sem=recv, device_id=device, device_id_type=MESH
    )


def arrived(buf, sem):
    pltpu.make_async_copy(buf, buf, sem).wait()


def far_first(u):
    y = u >> 2
    dy = jnp.where(y == 0, 2, jnp.where(y == 1, 1, jnp.where(y == 2, 3, 0)))
    return 1 - (u & 1), 1 - ((u >> 1) & 1), dy


def other_chip(m, dx, dy):
    return (((m >> 2) ^ dx) << 2) + (((m & 3) + dy) & 3)


def far_z(r, t):
    k = (t + 1) >> 1
    return ((r >> 1) + jnp.where((t & 1) == 1, 4 - k, 4 + k)) & 7


def parity(r):
    return (r >> 1) & 1


def place(r):
    return ((r >> 2) & 1) * 2 + (r & 1)


def to_channels(src, dst, send, recv, r, c):
    half, m, core = r // 8, c // 2, lax.rem(c, 2)
    own = r * 8 + m

    def body(s, _):
        dxh, dxl, dy = far_first(s >> 3)
        r2 = far_z(r, s & 7) * 2 + ((r & 1) ^ dxh)
        m2 = other_chip(m, dxl, dy)
        remote(src.at[r2 * 8 + m2], dst, send, recv, (r2, m2 * 2 + half)).start()
        return 0

    lax.fori_loop(0, 127, body, 0)

    @pl.when(core == half)
    def _():
        pltpu.make_async_copy(src.at[own], dst, recv).start()

    @pl.when(core != half)
    def _():
        remote(src.at[own], dst, send, recv, (r, m * 2 + half)).start()


def to_cells(src, dst, group, send, recv, r, c):
    half, m, core = r // 8, c // 2, lax.rem(c, 2)
    channel = r * 8 + m
    mine = place(r)
    base = core * 8 + group * 2

    def body(s, _):
        _, dxl, dy = far_first((s >> 3) * 2)
        w = mine ^ 3 ^ (s & 3)
        c2 = other_chip(m, dxl, dy) * 2 + (core ^ 1 ^ ((s >> 2) & 1))
        remote(src.at[w, c2], dst.at[channel], send, recv, (base + (w >> 1) * 4 + (w & 1), c2)).start()
        return 0

    lax.fori_loop(0, 63, body, 0)
    to_self = jnp.logical_and(core == half, parity(r) == group)

    @pl.when(to_self)
    def _():
        pltpu.make_async_copy(src.at[mine, c], dst.at[channel], recv).start()

    @pl.when(jnp.logical_not(to_self))
    def _():
        remote(src.at[mine, c], dst.at[channel], send, recv, (base + (mine >> 1) * 4 + (mine & 1), c)).start()


def sent(src, send, r, c):
    same = r // 8 == lax.rem(c, 2)

    @pl.when(same)
    def _():
        arrived(src.at[pl.ds(0, 127)], send)

    @pl.when(jnp.logical_not(same))
    def _():
        arrived(src, send)


def sent_half(group, src, send, r, c):
    to_self = jnp.logical_and(lax.rem(c, 2) == r // 8, parity(r) == group)

    @pl.when(to_self)
    def _():
        arrived(src.at[pl.ds(0, 63)], send)

    @pl.when(jnp.logical_not(to_self))
    def _():
        arrived(src.at[pl.ds(0, 64)], send)


def along_plane(pick, dst, send, recv, r, c):
    core, m = c & 1, c >> 1
    me = (r & 1) * 16 + c
    pltpu.make_async_copy(pick(me), dst.at[me], recv).start()

    def body(s, _):
        dxh, dxl, dy = far_first(s >> 1)
        r2 = r ^ dxh
        c2 = other_chip(m, dxl, dy) * 2 + (core ^ 1 ^ (s & 1))
        remote(pick((r2 & 1) * 16 + c2), dst.at[me], send, recv, (r2, c2)).start()
        return 0

    lax.fori_loop(0, 31, body, 0)


def along_z(src, dst, send, recv, r, c):
    pltpu.make_async_copy(src, dst.at[r >> 1], recv).start()

    def body(s, _):
        remote(src, dst.at[r >> 1], send, recv, (far_z(r, s) * 2 + (r & 1), c)).start()
        return 0

    lax.fori_loop(0, 7, body, 0)


def valid_of(place, counts, skip):
    start = jnp.int32(0)
    valid = jnp.zeros(place.shape, F32)
    for n in range(counts.shape[0]):
        end = start + counts[n]
        inside = (place >= start) & (place < end) & (place - start >= skip[n])
        valid = jnp.where(inside, 1.0, valid)
        start = end
    return valid


def kernel(
    counts_h, skip_h, pair_h, cot_h, w_proj_h, w_gin_h, w_gout_h, w_out_h,
    upd_h, gpair_h, sums_h,
    counts, skip, pair, cot, w_proj, w_gin, w_gout, w_out, upd, gpair,
    wp_t, wg_t, wgo_t, wo_t, perm,
    xh, xb, rstd, pt, ctt, dxl, gate, slope, go, dgo, dtn, dyb, tnb, dsb, dpb, dgb,
    f_left, f_right, f_mat, left, right, dmat, partial, got,
    m_r, m_l, m_t, m_d, m_dl, m_dr,
    b_r, b_l, b_t, b_d, b_dl, b_dr,
    s_src, s_got, s_part, s_parts, s_tot, s_out, s_sum,
    send, recv, load,
):
    pending = []

    r, c = lax.axis_index("row"), lax.axis_index("col")
    core = lax.rem(c, 2)
    sibling = (r, c + 1 - 2 * core)
    loads = [
        pltpu.make_async_copy(a, b, load.at[n])
        for n, (a, b) in enumerate([
            (pair_h, pair), (w_proj_h, w_proj), (w_gin_h, w_gin), (counts_h, counts), (skip_h, skip),
            (cot_h, cot), (w_gout_h, w_gout), (w_out_h, w_out),
        ])
    ]
    for copy in loads:
        copy.start()
    greet(r, c)
    i0 = lax.broadcasted_iota(jnp.int32, (128, 128), 0)
    i1 = lax.broadcasted_iota(jnp.int32, (128, 128), 1)
    eye = jnp.where(i0 == i1, 1.0, 0.0).astype(BF)
    for copy in loads[:5]:
        copy.wait()
    wp_t[...] = w_proj[...].astype(F32).T.astype(BF)
    wg_t[...] = w_gin[...].astype(F32).T.astype(BF)

    def normed(q, _):
        p = pair[pl.ds(q * 4, 4)].reshape(128, 128)
        p_t = dot(eye, p, ((1,), (1,)))
        pt[q] = p_t
        mean = jnp.mean(p_t, axis=0, keepdims=True)
        dev = p_t - mean
        var = jnp.mean(dev * dev, axis=0, keepdims=True)
        rs = 1.0 / jnp.sqrt(var + EPS)
        x_f = dev * rs
        xh[q] = x_f
        rstd[q] = jnp.broadcast_to(rs, (8, 128))
        xb[:, pl.ds(pl.multiple_of(q * 128, 128), 128)] = x_f.astype(BF)
        return 0

    def project(lo, f):
        def body(q, _):
            x = xb[:, pl.ds(pl.multiple_of(q * 128, 128), 128)]
            s = dot(wp_t[lo:lo + 128, :], x)
            sig = jax.nn.sigmoid(dot(wg_t[lo:lo + 128, :], x))
            lane = lax.broadcasted_iota(jnp.int32, (1, 128), 1)
            mask = valid_of(r * 32 + q * 4 + lane // 32, counts, skip) * valid_of(c * 32 + lane % 32, counts, skip)
            open_ = mask * sig
            both = open_ * s
            gate[q, lo:lo + 128] = open_
            slope[q, lo:lo + 128] = both * (1.0 - sig)
            f[pl.ds(q, 128, stride=8), :] = both
            return 0

        lax.fori_loop(0, 8, body, 0, unroll=4)

    lax.fori_loop(0, 8, normed, 0, unroll=4)
    project(128, f_right)
    m_r[...] = f_right[...].reshape(128, 8, 128).astype(BF)
    greeted(r, c)
    group, spot = parity(r), place(r)
    to_channels(m_r, b_r.at[r & 7, c], send.at[0], recv.at[0], r, c)
    pending.append(lambda: sent(m_r, send.at[0], r, c))
    j0 = lax.broadcasted_iota(jnp.int32, (512, 512), 0)
    j1 = lax.broadcasted_iota(jnp.int32, (512, 512), 1)
    swapped = ((j0 >> 5) & 3) * 128 + (j0 >> 7) * 32 + (j0 & 31)
    perm[...] = jnp.where(swapped == j1, 1.0, 0.0).astype(BF)
    project(0, f_left)
    m_l[...] = f_left[...].reshape(128, 8, 128).astype(BF)

    @pl.when(group == 0)
    def _():
        to_channels(m_l, b_l.at[0, spot, c], send.at[1], recv.at[1], r, c)

    def before(q, _):
        at = pl.ds(pl.multiple_of(q * 128, 128), 128)
        ct = dot(eye, cot[pl.ds(q * 4, 4)].reshape(128, 128), ((1,), (1,)))
        ctt[q] = ct
        g = jax.nn.sigmoid(dot(wgo_t[...], xb[:, at]))
        go[q] = g
        dy_f = ct * g
        dgo[q] = dy_f * (1.0 - g)
        dy = dy_f.astype(BF)
        dyb[:, at] = dy
        dt = dot(w_out[...], dy)
        dtn[q] = dt - jnp.mean(dt, axis=0, keepdims=True)
        return 0


    for copy in loads[5:]:
        copy.wait()
    wgo_t[...] = w_gout[...].astype(F32).T.astype(BF)
    wo_t[...] = w_out[...].astype(F32).T.astype(BF)
    lax.fori_loop(0, 8, before, 0, unroll=2)

    @pl.when(group == 1)
    def _():
        to_channels(m_l, b_l.at[1, spot, c], send.at[1], recv.at[2], r, c)

    pending.append(lambda: sent(m_r, send.at[1], r, c))

    def turned(buf):
        n_rows = buf.shape[0] * 8
        rows = []
        for g in range(4):
            cols = [buf[:, 4 * g + n].astype(F32).reshape(n_rows, 128).astype(BF) for n in range(4)]
            rows.append(jnp.concatenate(cols, axis=1))
        return dot(jnp.concatenate(rows, axis=0), perm[...])

    def natural(buf, out):
        o = turned(buf)
        for g in range(4):
            for a in range(4):
                f_mat[pl.ds(g * 256 + a, 64, stride=4), :] = o[g * 64:(g + 1) * 64, a * 128:(a + 1) * 128]
        for g in range(4):
            out[:, g * 128:(g + 1) * 128] = f_mat[g * 256:(g + 1) * 256].astype(BF)

    def matrix(buf, out):
        o = turned(buf)
        for g in range(4):
            for a in range(4):
                out[a * 32:(a + 1) * 32, g * 128:(g + 1) * 128] = o[g * 32:(g + 1) * 32, a * 128:(a + 1) * 128].astype(BF)

    def spread(block):
        rows = [jnp.concatenate([block(a, g).astype(BF) for a in range(4)], axis=1) for g in range(4)]
        return dot(jnp.concatenate(rows, axis=0), perm[...])

    def messages(mat, out):
        o = spread(lambda a, g: mat[a * 32:(a + 1) * 32, g * 128:(g + 1) * 128])
        for g in range(4):
            for n in range(4):
                out[:, 4 * g + n] = o[g * 32:(g + 1) * 32, n * 128:(n + 1) * 128].reshape(4, 8, 128).astype(BF)

    def natural_messages(mat, out):
        for g in range(4):
            f_mat[g * 256:(g + 1) * 256] = mat[:, g * 128:(g + 1) * 128]
        o = spread(lambda a, g: f_mat[pl.ds(g * 256 + a, 64, stride=4), :])
        for g in range(4):
            for n in range(4):
                p = o[g * 64:(g + 1) * 64, n * 128:(n + 1) * 128].reshape(2, 2, 2, 8, 128).astype(BF)
                for x in range(2):
                    out[x, :, 4 * g + n] = p[:, x].reshape(4, 8, 128)

    def scatter(n):
        along_plane(lambda k: s_src.at[n, k], s_got.at[n], send.at[8 + n], recv.at[10 + n], r, c)
        pending.append(lambda: arrived(s_got.at[n, pl.ds(0, 31)], send.at[8 + n]))

    def share(n):
        arrived(s_got.at[n], recv.at[10 + n])
        s_part[n] = jnp.sum(s_got[n].astype(F32), axis=0).astype(BF)
        along_z(s_part.at[n], s_parts.at[n], send.at[11 + n], recv.at[13 + n], r, c)
        pending.append(lambda: arrived(s_parts.at[n, pl.ds(0, 7)], send.at[11 + n]))

    def gather(n):
        arrived(s_parts.at[n], recv.at[13 + n])
        s_tot[n] = (jnp.sum(s_parts[n].astype(F32), axis=0) * (1.0 / 512)).astype(BF)
        along_plane(lambda k: s_tot.at[n], s_out.at[n], send.at[14 + n], recv.at[16 + n], r, c)
        pending.append(lambda: arrived(s_got.at[n, pl.ds(0, 31)], send.at[14 + n]))

    outs = []

    def put(src, dst, n):
        copy = pltpu.make_async_copy(src, dst, load.at[8 + n])
        copy.start()
        outs.append(copy)

    mine = right.at[pl.ds(pl.multiple_of(core * 256, 256), 256)]
    arrived(b_r, recv.at[0])
    natural(b_r, mine)
    swap = remote(mine, mine, send.at[6], recv.at[8], sibling)
    swap.start()
    pending.append(swap.wait_send)
    for x in range(2):
        arrived(b_l.at[x], recv.at[1 + x])
        at = pl.ds(x * 128, 128)
        matrix(b_l.at[x], left.at[at])
        if x == 0:
            swap.wait_recv()
        messages(dot(left[at], right[...], ((1,), (1,))), m_t.at[x])
        to_cells(m_t.at[x], b_t, x, send.at[2 + 15 * x], recv.at[3], r, c)
    pending.append(lambda: sent_half(1, m_r, send.at[17], r, c))
    pending.append(lambda: sent_half(0, m_r, send.at[2], r, c))
    pending.append(lambda: sent(m_r, send.at[4], r, c))
    arrived(b_t, recv.at[3])
    f_left[...] = b_t[...].astype(F32).reshape(1024, 128)

    def middle(q, _):
        at = pl.ds(pl.multiple_of(q * 128, 128), 128)
        t = f_left[pl.ds(q, 128, stride=8), :]
        dev = t - jnp.mean(t, axis=0, keepdims=True)
        rs = 1.0 / jnp.sqrt(jnp.mean(dev * dev, axis=0, keepdims=True) + EPS)
        that = dev * rs
        tnb[:, at] = that.astype(BF)
        d = dtn[q]
        f_right[pl.ds(q, 128, stride=8), :] = rs * (d - that * jnp.mean(d * that, axis=0, keepdims=True))
        return 0

    lax.fori_loop(0, 8, middle, 0, unroll=4)
    m_d[...] = f_right[...].reshape(128, 8, 128).astype(BF)
    to_channels(m_d, b_d.at[group, spot, c], send.at[3], recv.at[4 + group], r, c)
    pending.append(lambda: sent(m_r, send.at[3], r, c))

    def after(q, _):
        at = pl.ds(pl.multiple_of(q * 128, 128), 128)
        y = dot(wo_t[...], tnb[:, at])
        dsb[:, at] = (dgo[q] * y).astype(BF)
        u = (pt[q] + go[q] * y).astype(BF)
        upd[pl.ds(q * 4, 4)] = dot(u, eye, ((0,), (0,))).astype(BF).reshape(4, 32, 128)
        return 0

    theirs = pl.ds(pl.multiple_of((1 - core) * 256, 256), 256)
    ours = pl.ds(pl.multiple_of(core * 256, 256), 256)
    cross = remote(partial, got, send.at[7], recv.at[9], sibling)
    for x in range(2):
        arrived(b_d.at[x], recv.at[4 + x])
        at = pl.ds(x * 128, 128)
        matrix(b_d.at[x], dmat.at[at])
        if x == 1:
            partial[...] = dot(dmat[:, theirs], left[...], ((0,), (0,))).astype(BF)
            cross.start()
        messages(dot(dmat[at], right[...]), m_dl.at[x])
        to_cells(m_dl.at[x], b_dl, x, send.at[4], recv.at[6], r, c)
    pending.append(cross.wait_send)
    part = dot(dmat[:, ours], left[...], ((0,), (0,)))
    cross.wait_recv()
    natural_messages(part + got[...].astype(F32), m_dr)
    for x in range(2):
        to_cells(m_dr.at[x], b_dr, x, send.at[5], recv.at[7], r, c)
    pending.append(lambda: sent(m_r, send.at[5], r, c))
    lax.fori_loop(0, 8, after, 0, unroll=2)
    put(upd, upd_h, 0)
    s_src[0, pl.ds(0, 16)] = dot(xb[...], dsb[...], ((1,), (1,))).reshape(16, 8, 128).astype(BF)
    s_src[0, pl.ds(16, 16)] = dot(tnb[...], dyb[...], ((1,), (1,))).reshape(16, 8, 128).astype(BF)
    scatter(0)

    def back(n, lo, f):
        def body(q, _):
            at = pl.ds(pl.multiple_of(q * 128, 128), 128)
            d = f[pl.ds(q, 128, stride=8), :]
            dpb[lo:lo + 128, at] = (d * gate[q, lo:lo + 128]).astype(BF)
            dgb[lo:lo + 128, at] = (d * slope[q, lo:lo + 128]).astype(BF)
            return 0

        lax.fori_loop(0, 8, body, 0, unroll=4)
        s_src[n, pl.ds(0, 16)] = dot(xb[...], dpb[lo:lo + 128, :], ((1,), (1,))).reshape(16, 8, 128).astype(BF)
        s_src[n, pl.ds(16, 16)] = dot(xb[...], dgb[lo:lo + 128, :], ((1,), (1,))).reshape(16, 8, 128).astype(BF)
        scatter(n)

    arrived(b_dl, recv.at[6])
    f_left[...] = b_dl[...].astype(F32).reshape(1024, 128)
    back(1, 0, f_left)

    def early(q, _):
        at = pl.ds(pl.multiple_of(q * 128, 128), 128)
        dxl[q] = (
            dot(w_proj[:, :128], dpb[:128, at]) + dot(w_gin[:, :128], dgb[:128, at]) + dot(w_gout[...], dsb[:, at])
        )
        return 0

    lax.fori_loop(0, 8, early, 0, unroll=2)
    arrived(b_dr, recv.at[7])
    f_right[...] = b_dr[...].astype(F32).reshape(1024, 128)
    back(2, 128, f_right)
    share(0)
    share(1)

    def last(q, _):
        at = pl.ds(pl.multiple_of(q * 128, 128), 128)
        dx = dxl[q] + dot(w_proj[:, 128:], dpb[128:, at]) + dot(w_gin[:, 128:], dgb[128:, at])
        x_f = xh[q]
        dx = dx - jnp.mean(dx, axis=0, keepdims=True) - x_f * jnp.mean(dx * x_f, axis=0, keepdims=True)
        u = (ctt[q] + rstd[q][:1] * dx).astype(BF)
        gpair[pl.ds(q * 4, 4)] = dot(u, eye, ((0,), (0,))).astype(BF).reshape(4, 32, 128)
        return 0

    lax.fori_loop(0, 2, last, 0, unroll=2)
    share(2)
    gather(0)
    gather(1)
    lax.fori_loop(2, 6, last, 0, unroll=2)

    def total(n):
        arrived(s_out.at[n], recv.at[16 + n])
        s_sum[n] = s_out[n].astype(F32)
        put(s_sum.at[n], sums_h.at[n], 2 + n)

    gather(2)
    lax.fori_loop(6, 8, last, 0, unroll=2)
    put(gpair, gpair_h, 1)
    total(0)
    total(1)
    for wait in pending:
        wait()
    total(2)
    for copy in outs:
        copy.wait()


def finish(upd, gpair, sums, upd_o, gpair_o, g_proj, g_gin, g_gout, g_out, upd_v, gpair_v, sums_v, sem):
    loads = [
        pltpu.make_async_copy(a, b, sem.at[n])
        for n, (a, b) in enumerate([(upd, upd_v), (gpair, gpair_v), (sums, sums_v)])
    ]
    for copy in loads:
        copy.start()
    flat = sums_v.reshape(6, 128, 128)
    left, right = pl.ds(0, 128), pl.ds(128, 128)
    pairs = [
        (upd_v, upd_o), (gpair_v, gpair_o), (flat.at[0], g_gout), (flat.at[1], g_out),
        (flat.at[2], g_proj.at[:, left]), (flat.at[3], g_gin.at[:, left]),
        (flat.at[4], g_proj.at[:, right]), (flat.at[5], g_gin.at[:, right]),
    ]
    stores = [pltpu.make_async_copy(a, b, sem.at[3 + n]) for n, (a, b) in enumerate(pairs)]
    for n, copy in enumerate(stores):
        if n < 3:
            loads[n].wait()
        copy.start()
    for copy in stores:
        copy.wait()


def shards(pair, cotangent, chain_counts, crop_skip, w_proj, w_gate_in, w_gate_out, w_out):
    hbm = pl.BlockSpec(memory_space=pl.ANY)
    v = pltpu.VMEM
    s = jax.ShapeDtypeStruct
    scratch = (
        [pltpu.SMEM((4,), jnp.int32)] * 2 + [v((32, 32, 128), BF)] * 2
        + [v((128, 256), BF)] * 2 + [v((128, 128), BF)] * 2 + [v((32, 32, 128), BF)] * 2
        + [v((256, 128), BF), v((256, 128), BF), v((128, 128), BF), v((128, 128), BF), v((512, 512), BF)]
        + [v((8, 128, 128), F32), v((128, 1024), BF), v((8, 8, 128), F32), v((8, 128, 128), F32), v((8, 128, 128), F32)]
        + [v((8, 128, 128), F32)]
        + [v((8, 256, 128), F32), v((8, 256, 128), F32)]
        + [v((8, 128, 128), F32)] * 3
        + [v((128, 1024), BF)] * 3
        + [v((256, 1024), BF)] * 2
        + [v((1024, 128), F32)] * 2
        + [v((1024, 128), F32), v((256, 512), BF), v((512, 512), BF), v((256, 512), BF)]
        + [v((256, 512), BF)] * 2
        + [v((128, 8, 128), BF)] * 2 + [v((2, 4, 16, 8, 128), BF)] + [v((128, 8, 128), BF)] + [v((2, 4, 16, 8, 128), BF)] * 2
        + [v((8, 16, 8, 128), BF), v((2, 4, 16, 8, 128), BF), v((128, 8, 128), BF), v((2, 4, 16, 8, 128), BF)]
        + [v((128, 8, 128), BF)] * 2
        + [v((3, 32, 8, 128), BF)] * 2 + [v((3, 8, 128), BF), v((3, 8, 8, 128), BF), v((3, 8, 128), BF)]
        + [v((3, 32, 8, 128), BF), v((3, 32, 8, 128), F32)]
        + [pltpu.SemaphoreType.DMA((18,)), pltpu.SemaphoreType.DMA((19,)), pltpu.SemaphoreType.DMA((13,))]
    )
    block = s((32, 32, 128), BF)
    wide, square = s((128, 256), F32), s((128, 128), F32)
    results = pl.pallas_call(
        kernel,
        out_shape=(block, block, s((3, 32, 8, 128), F32)),
        in_specs=[hbm] * 8,
        out_specs=(hbm,) * 3,
        scratch_shapes=scratch,
        compiler_params=pltpu.CompilerParams(collective_id=1, has_side_effects=True, vmem_limit_bytes=60 << 20),
    )(chain_counts, crop_skip, pair, cotangent, w_proj, w_gate_in, w_gate_out, w_out)
    return pl.pallas_call(
        finish,
        out_shape=(block, block, wide, wide, square, square),
        in_specs=[hbm] * 3,
        out_specs=(hbm,) * 6,
        scratch_shapes=[v(block.shape, BF)] * 2 + [v((3, 32, 8, 128), F32), pltpu.SemaphoreType.DMA((11,))],
        compiler_params=pltpu.CompilerParams(vmem_limit_bytes=60 << 20),
    )(*results)


def solution(mesh):
    in_specs = (P("row", "col", None), P("row", "col", None), P(), P(), P(), P(), P(), P())
    out_specs = (P("row", "col", None), P("row", "col", None), P(), P(), P(), P())
    return jax.shard_map(shards, mesh=mesh, in_specs=in_specs, out_specs=out_specs, check_vma=False)
```

time: 88.1 us -> 85.9 us (0.975)
  Pallas kernels: 87.3 us -> 85.2 us
    pallas_call x1, Pallas kernels: 85.3 us -> 83.2 us  [shards(): pl.pallas_call(kernel, out_shape=(block, block, s((3, 32, 8, 128), F32)),...]
where the time goes in v5:
time: 85.9 us; the launch traced here: 85.8 us
  Pallas kernels  85.2 us (99%)
    pallas_call x1, Pallas kernels, shards(): pl.pallas_call(kernel, out_shape=(block, block, s((3, 32, 8, 128), F32)),...  83.2 us
    pallas_call x1, Pallas kernels, shards(): pl.pallas_call(finish, out_shape=(block, block, wide, wide, square, squar...  1.99 us

profile of v5, /device:TPU:1, one launch (start us, length us, event | category | flops | bytes accessed | tf_op | source)
XLA Modules:
  0.0 85.8 jit_solution(1209405519180919719)
XLA Ops:
  0.6 83.2 %shard_map.127 = (bf16[32,32,128]{2,1,0:T(8,128)(2,1)}, bf16[32,32,128]{2,1,0:T(8,128)(2,1)}, f32[3,32,8,128]{3,2,1,0:T(8,128)}) custom-call(s32[4]{0:T(128)} %counts_h.1, s32[4]{0:T(128)} %skip_h.1, bf16[32,32,128]{2,1,0:T(8,128)(2,1)} %pair_h.1, bf16[32,32,128]{2,1,0:T(8,128)(2,1)} %cot_h.1, bf16[128,256]{1,0:T(8,128)(2,1)} %w_proj_h.1, ...), custom_call_target="tpu_custom_call" | custom-call | tf_op jit(solution)/shard_map/pallas_call | solution.py:546
  83.8 2.0 %shard_map.128 = (bf16[32,32,128]{2,1,0:T(8,128)(2,1)}, bf16[32,32,128]{2,1,0:T(8,128)(2,1)}, f32[128,256]{1,0:T(8,128)}, f32[128,256]{1,0:T(8,128)}, f32[128,128]{1,0:T(8,128)}, /*index=5*/f32[128,128]{1,0:T(8,128)}) custom-call(bf16[32,32,128]{2,1,0:T(8,128)(2,1)} %get-tuple-element.9.upd, bf16[32,32,128]{2,1,0:T(8,128)(2,1)} %get-tuple-element.10.gpair, ...), custom_call_target="tpu_custom_call" | custom-call | tf_op jit(solution)/shard_map/pallas_call | solution.py:554

commit v6 on v5

--- a/solution.py
+++ b/solution.py
@@ -166,11 +166,25 @@
     lax.fori_loop(0, 31, body, 0)
 
 
+def to_plane(src, dst, send, recv, r, c):
+    me = (r & 1) * 16 + c
+    pltpu.make_async_copy(src, dst.at[me], recv).start()
+
+    def body(s, _):
+        k = s + jnp.where(s >= (me ^ 1), 1, 0)
+        p = k ^ 1
+        remote(src, dst.at[me], send, recv, ((r & 14) + (p >> 4), p & 15)).start()
+        return 0
+
+    lax.fori_loop(0, 31, body, 0)
+
+
 def along_z(src, dst, send, recv, r, c):
     pltpu.make_async_copy(src, dst.at[r >> 1], recv).start()
 
     def body(s, _):
-        remote(src, dst.at[r >> 1], send, recv, (far_z(r, s) * 2 + (r & 1), c)).start()
+        z = s + jnp.where(s >= (r >> 1), 1, 0)
+        remote(src, dst.at[r >> 1], send, recv, (z * 2 + (r & 1), c)).start()
         return 0
 
     lax.fori_loop(0, 7, body, 0)
@@ -196,10 +210,11 @@
     f_left, f_right, f_mat, left, right, dmat, partial, got,
     m_r, m_l, m_t, m_d, m_dl, m_dr,
     b_r, b_l, b_t, b_d, b_dl, b_dr,
-    s_src, s_got, s_part, s_parts, s_tot, s_out, s_sum,
+    a_src, a_got, a_part, a_parts, a_tot, a_out, s_src, s_got, s_part, s_parts, s_tot, s_out, s_sum,
     send, recv, load,
 ):
     pending = []
+    groups = ((a_src, a_got, a_part, a_parts, a_tot, a_out), (s_src, s_got, s_part, s_parts, s_tot, s_out))
 
     r, c = lax.axis_index("row"), lax.axis_index("col")
     core = lax.rem(c, 2)
@@ -254,7 +269,7 @@
 
     lax.fori_loop(0, 8, normed, 0, unroll=4)
     project(128, f_right)
-    m_r[...] = f_right[...].reshape(128, 8, 128).astype(BF)
+    m_r[...] = f_right[:1024].reshape(128, 8, 128).astype(BF)
     greeted(r, c)
     group, spot = parity(r), place(r)
     to_channels(m_r, b_r.at[r & 7, c], send.at[0], recv.at[0], r, c)
@@ -264,7 +279,7 @@
     swapped = ((j0 >> 5) & 3) * 128 + (j0 >> 7) * 32 + (j0 & 31)
     perm[...] = jnp.where(swapped == j1, 1.0, 0.0).astype(BF)
     project(0, f_left)
-    m_l[...] = f_left[...].reshape(128, 8, 128).astype(BF)
+    m_l[...] = f_left[:1024].reshape(128, 8, 128).astype(BF)
 
     @pl.when(group == 0)
     def _():
@@ -340,20 +355,23 @@
                     out[x, :, 4 * g + n] = p[:, x].reshape(4, 8, 128)
 
     def scatter(n):
-        along_plane(lambda k: s_src.at[n, k], s_got.at[n], send.at[8 + n], recv.at[10 + n], r, c)
-        pending.append(lambda: arrived(s_got.at[n, pl.ds(0, 31)], send.at[8 + n]))
+        src, got = groups[n][:2]
+        along_plane(lambda k: src.at[k], got, send.at[8 + n], recv.at[10 + n], r, c)
+        pending.append(lambda: arrived(got.at[pl.ds(0, 31)], send.at[8 + n]))
 
     def share(n):
-        arrived(s_got.at[n], recv.at[10 + n])
-        s_part[n] = jnp.sum(s_got[n].astype(F32), axis=0).astype(BF)
-        along_z(s_part.at[n], s_parts.at[n], send.at[11 + n], recv.at[13 + n], r, c)
-        pending.append(lambda: arrived(s_parts.at[n, pl.ds(0, 7)], send.at[11 + n]))
+        got, part, parts = groups[n][1:4]
+        arrived(got, recv.at[10 + n])
+        part[...] = jnp.sum(got[...].astype(F32), axis=0).astype(BF)
+        along_z(part, parts, send.at[11 + n], recv.at[13 + n], r, c)
+        pending.append(lambda: arrived(parts.at[pl.ds(0, 7)], send.at[11 + n]))
 
     def gather(n):
-        arrived(s_parts.at[n], recv.at[13 + n])
-        s_tot[n] = (jnp.sum(s_parts[n].astype(F32), axis=0) * (1.0 / 512)).astype(BF)
-        along_plane(lambda k: s_tot.at[n], s_out.at[n], send.at[14 + n], recv.at[16 + n], r, c)
-        pending.append(lambda: arrived(s_got.at[n, pl.ds(0, 31)], send.at[14 + n]))
+        parts, tot, out = groups[n][3:]
+        arrived(parts, recv.at[13 + n])
+        tot[...] = (jnp.sum(parts[...].astype(F32), axis=0) * (1.0 / 512)).astype(BF)
+        to_plane(tot, out, send.at[14 + n], recv.at[16 + n], r, c)
+        pending.append(lambda: arrived(out.at[pl.ds(0, 31)], send.at[14 + n]))
 
     outs = []
 
@@ -380,7 +398,7 @@
     pending.append(lambda: sent_half(0, m_r, send.at[2], r, c))
     pending.append(lambda: sent(m_r, send.at[4], r, c))
     arrived(b_t, recv.at[3])
-    f_left[...] = b_t[...].astype(F32).reshape(1024, 128)
+    f_left[:1024] = b_t[...].astype(F32).reshape(1024, 128)
 
     def middle(q, _):
         at = pl.ds(pl.multiple_of(q * 128, 128), 128)
@@ -394,7 +412,7 @@
         return 0
 
     lax.fori_loop(0, 8, middle, 0, unroll=4)
-    m_d[...] = f_right[...].reshape(128, 8, 128).astype(BF)
+    m_d[...] = f_right[:1024].reshape(128, 8, 128).astype(BF)
     to_channels(m_d, b_d.at[group, spot, c], send.at[3], recv.at[4 + group], r, c)
     pending.append(lambda: sent(m_r, send.at[3], r, c))
 
@@ -427,11 +445,9 @@
     pending.append(lambda: sent(m_r, send.at[5], r, c))
     lax.fori_loop(0, 8, after, 0, unroll=2)
     put(upd, upd_h, 0)
-    s_src[0, pl.ds(0, 16)] = dot(xb[...], dsb[...], ((1,), (1,))).reshape(16, 8, 128).astype(BF)
-    s_src[0, pl.ds(16, 16)] = dot(tnb[...], dyb[...], ((1,), (1,))).reshape(16, 8, 128).astype(BF)
-    scatter(0)
-
-    def back(n, lo, f):
+    a_src[pl.ds(0, 16), 0] = dot(xb[...], dsb[...], ((1,), (1,))).reshape(16, 8, 128).astype(BF)
+    a_src[pl.ds(16, 16), 0] = dot(tnb[...], dyb[...], ((1,), (1,))).reshape(16, 8, 128).astype(BF)
+    def back(lo, f):
         def body(q, _):
             at = pl.ds(pl.multiple_of(q * 128, 128), 128)
             d = f[pl.ds(q, 128, stride=8), :]
@@ -440,13 +456,14 @@
             return 0
 
         lax.fori_loop(0, 8, body, 0, unroll=4)
-        s_src[n, pl.ds(0, 16)] = dot(xb[...], dpb[lo:lo + 128, :], ((1,), (1,))).reshape(16, 8, 128).astype(BF)
-        s_src[n, pl.ds(16, 16)] = dot(xb[...], dgb[lo:lo + 128, :], ((1,), (1,))).reshape(16, 8, 128).astype(BF)
-        scatter(n)
+        return tuple(
+            dot(xb[...], d[lo:lo + 128, :], ((1,), (1,))).reshape(16, 8, 128).astype(BF) for d in (dpb, dgb)
+        )
 
     arrived(b_dl, recv.at[6])
-    f_left[...] = b_dl[...].astype(F32).reshape(1024, 128)
-    back(1, 0, f_left)
+    f_left[:1024] = b_dl[...].astype(F32).reshape(1024, 128)
+    a_src[pl.ds(0, 16), 1], a_src[pl.ds(16, 16), 1] = back(0, f_left)
+    scatter(0)
 
     def early(q, _):
         at = pl.ds(pl.multiple_of(q * 128, 128), 128)
@@ -457,10 +474,10 @@
 
     lax.fori_loop(0, 8, early, 0, unroll=2)
     arrived(b_dr, recv.at[7])
-    f_right[...] = b_dr[...].astype(F32).reshape(1024, 128)
-    back(2, 128, f_right)
+    f_right[:1024] = b_dr[...].astype(F32).reshape(1024, 128)
+    s_src[pl.ds(0, 16)], s_src[pl.ds(16, 16)] = back(128, f_right)
+    scatter(1)
     share(0)
-    share(1)
 
     def last(q, _):
         at = pl.ds(pl.multiple_of(q * 128, 128), 128)
@@ -472,24 +489,22 @@
         return 0
 
     lax.fori_loop(0, 2, last, 0, unroll=2)
-    share(2)
+    share(1)
     gather(0)
+    lax.fori_loop(2, 6, last, 0, unroll=2)
+
     gather(1)
-    lax.fori_loop(2, 6, last, 0, unroll=2)
-
-    def total(n):
-        arrived(s_out.at[n], recv.at[16 + n])
-        s_sum[n] = s_out[n].astype(F32)
-        put(s_sum.at[n], sums_h.at[n], 2 + n)
-
-    gather(2)
     lax.fori_loop(6, 8, last, 0, unroll=2)
     put(gpair, gpair_h, 1)
-    total(0)
-    total(1)
+    arrived(a_out, recv.at[16])
+    for n in range(2):
+        s_sum[n] = a_out[:, n].astype(F32)
+        put(s_sum.at[n], sums_h.at[n], 2 + n)
     for wait in pending:
         wait()
-    total(2)
+    arrived(s_out, recv.at[17])
+    s_sum[2] = s_out[...].astype(F32)
+    put(s_sum.at[2], sums_h.at[2], 4)
     for copy in outs:
         copy.wait()
 
@@ -531,14 +546,15 @@
         + [v((8, 128, 128), F32)] * 3
         + [v((128, 1024), BF)] * 3
         + [v((256, 1024), BF)] * 2
-        + [v((1024, 128), F32)] * 2
-        + [v((1024, 128), F32), v((256, 512), BF), v((512, 512), BF), v((256, 512), BF)]
+        + [v((1032, 128), F32)] * 2
+        + [v((1032, 128), F32), v((256, 512), BF), v((512, 512), BF), v((256, 512), BF)]
         + [v((256, 512), BF)] * 2
         + [v((128, 8, 128), BF)] * 2 + [v((2, 4, 16, 8, 128), BF)] + [v((128, 8, 128), BF)] + [v((2, 4, 16, 8, 128), BF)] * 2
         + [v((8, 16, 8, 128), BF), v((2, 4, 16, 8, 128), BF), v((128, 8, 128), BF), v((2, 4, 16, 8, 128), BF)]
         + [v((128, 8, 128), BF)] * 2
-        + [v((3, 32, 8, 128), BF)] * 2 + [v((3, 8, 128), BF), v((3, 8, 8, 128), BF), v((3, 8, 128), BF)]
-        + [v((3, 32, 8, 128), BF), v((3, 32, 8, 128), F32)]
+        + [v((32, 2, 8, 128), BF)] * 2 + [v((2, 8, 128), BF), v((8, 2, 8, 128), BF), v((2, 8, 128), BF)]
+        + [v((32, 2, 8, 128), BF)] + [v((32, 8, 128), BF)] * 2
+        + [v((8, 128), BF), v((8, 8, 128), BF), v((8, 128), BF), v((32, 8, 128), BF), v((3, 32, 8, 128), F32)]
         + [pltpu.SemaphoreType.DMA((18,)), pltpu.SemaphoreType.DMA((19,)), pltpu.SemaphoreType.DMA((13,))]
     )
     block = s((32, 32, 128), BF)

time: 85.9 us -> 85.8 us (level)
  no operation moved by 1% of the time
where the time goes in v6:
time: 85.8 us; the launch traced here: 85.7 us
  Pallas kernels  85 us (99%)
    pallas_call x1, Pallas kernels, shards(): pl.pallas_call(kernel, out_shape=(block, block, s((3, 32, 8, 128), F32)),...  83 us
    pallas_call x1, Pallas kernels, shards(): pl.pallas_call(finish, out_shape=(block, block, wide, wide, square, squar...  1.99 us

profile of v6, /device:TPU:1, one launch (start us, length us, event | category | flops | bytes accessed | tf_op | source)
XLA Modules:
  0.0 85.7 jit_solution(16650063407445979224)
XLA Ops:
  0.6 83.0 %shard_map.127 = (bf16[32,32,128]{2,1,0:T(8,128)(2,1)}, bf16[32,32,128]{2,1,0:T(8,128)(2,1)}, f32[3,32,8,128]{3,2,1,0:T(8,128)}) custom-call(s32[4]{0:T(128)} %counts_h.1, s32[4]{0:T(128)} %skip_h.1, bf16[32,32,128]{2,1,0:T(8,128)(2,1)} %pair_h.1, bf16[32,32,128]{2,1,0:T(8,128)(2,1)} %cot_h.1, bf16[128,256]{1,0:T(8,128)(2,1)} %w_proj_h.1, ...), custom_call_target="tpu_custom_call" | custom-call | tf_op jit(solution)/shard_map/pallas_call | solution.py:562
  83.7 2.0 %shard_map.128 = (bf16[32,32,128]{2,1,0:T(8,128)(2,1)}, bf16[32,32,128]{2,1,0:T(8,128)(2,1)}, f32[128,256]{1,0:T(8,128)}, f32[128,256]{1,0:T(8,128)}, f32[128,128]{1,0:T(8,128)}, /*index=5*/f32[128,128]{1,0:T(8,128)}) custom-call(bf16[32,32,128]{2,1,0:T(8,128)(2,1)} %get-tuple-element.9.upd, bf16[32,32,128]{2,1,0:T(8,128)(2,1)} %get-tuple-element.10.gpair, ...), custom_call_target="tpu_custom_call" | custom-call | tf_op jit(solution)/shard_map/pallas_call | solution.py:570

commit v7 on v6

--- a/solution.py
+++ b/solution.py
@@ -281,9 +281,8 @@
     project(0, f_left)
     m_l[...] = f_left[:1024].reshape(128, 8, 128).astype(BF)
 
-    @pl.when(group == 0)
-    def _():
-        to_channels(m_l, b_l.at[0, spot, c], send.at[1], recv.at[1], r, c)
+    to_channels(m_l, b_l.at[group, spot, c], send.at[1], recv.at[1 + group], r, c)
+    pending.append(lambda: sent(m_r, send.at[1], r, c))
 
     def before(q, _):
         at = pl.ds(pl.multiple_of(q * 128, 128), 128)
@@ -300,18 +299,6 @@
         return 0
 
 
-    for copy in loads[5:]:
-        copy.wait()
-    wgo_t[...] = w_gout[...].astype(F32).T.astype(BF)
-    wo_t[...] = w_out[...].astype(F32).T.astype(BF)
-    lax.fori_loop(0, 8, before, 0, unroll=2)
-
-    @pl.when(group == 1)
-    def _():
-        to_channels(m_l, b_l.at[1, spot, c], send.at[1], recv.at[2], r, c)
-
-    pending.append(lambda: sent(m_r, send.at[1], r, c))
-
     def turned(buf):
         n_rows = buf.shape[0] * 8
         rows = []
@@ -386,6 +373,12 @@
     swap = remote(mine, mine, send.at[6], recv.at[8], sibling)
     swap.start()
     pending.append(swap.wait_send)
+
+    for copy in loads[5:]:
+        copy.wait()
+    wgo_t[...] = w_gout[...].astype(F32).T.astype(BF)
+    wo_t[...] = w_out[...].astype(F32).T.astype(BF)
+    lax.fori_loop(0, 8, before, 0, unroll=2)
     for x in range(2):
         arrived(b_l.at[x], recv.at[1 + x])
         at = pl.ds(x * 128, 128)

time: 85.8 us -> 85.8 us (level)
  no operation moved by 1% of the time
where the time goes in v7:
time: 85.8 us; the launch traced here: 85.7 us
  Pallas kernels  85.1 us (99%)
    pallas_call x1, Pallas kernels, shards(): pl.pallas_call(kernel, out_shape=(block, block, s((3, 32, 8, 128), F32)),...  83.1 us
    pallas_call x1, Pallas kernels, shards(): pl.pallas_call(finish, out_shape=(block, block, wide, wide, square, squar...  1.99 us

profile of v7, /device:TPU:1, one launch (start us, length us, event | category | flops | bytes accessed | tf_op | source)
XLA Modules:
  0.0 85.7 jit_solution(16033782526153265517)
XLA Ops:
  0.6 83.1 %shard_map.127 = (bf16[32,32,128]{2,1,0:T(8,128)(2,1)}, bf16[32,32,128]{2,1,0:T(8,128)(2,1)}, f32[3,32,8,128]{3,2,1,0:T(8,128)}) custom-call(s32[4]{0:T(128)} %counts_h.1, s32[4]{0:T(128)} %skip_h.1, bf16[32,32,128]{2,1,0:T(8,128)(2,1)} %pair_h.1, bf16[32,32,128]{2,1,0:T(8,128)(2,1)} %cot_h.1, bf16[128,256]{1,0:T(8,128)(2,1)} %w_proj_h.1, ...), custom_call_target="tpu_custom_call" | custom-call | tf_op jit(solution)/shard_map/pallas_call | solution.py:555
  83.7 2.0 %shard_map.128 = (bf16[32,32,128]{2,1,0:T(8,128)(2,1)}, bf16[32,32,128]{2,1,0:T(8,128)(2,1)}, f32[128,256]{1,0:T(8,128)}, f32[128,256]{1,0:T(8,128)}, f32[128,128]{1,0:T(8,128)}, /*index=5*/f32[128,128]{1,0:T(8,128)}) custom-call(bf16[32,32,128]{2,1,0:T(8,128)(2,1)} %get-tuple-element.9.upd, bf16[32,32,128]{2,1,0:T(8,128)(2,1)} %get-tuple-element.10.gpair, ...), custom_call_target="tpu_custom_call" | custom-call | tf_op jit(solution)/shard_map/pallas_call | solution.py:563
